TPU v7x, 128 devices: a whole 4x4x4 slice. The times are simulated.
128 devices in a mesh: dp: 8 (over y, x_lo), tensor: 16 (over z, x_hi, core).
Axes of the slice: x: 4 (x_hi: 2, x_lo: 2; x = x_hi * 2 + x_lo), y: 4, z: 4, core: 2. Of those that a mesh axis runs over, the one named last changes fastest.
Arguments:
- tokens: bfloat16 [1280, 4096], P(('dp', 'tensor')), may hold values from -6 to 6
- grad_out: bfloat16 [1280, 4096], P(('dp', 'tensor')), may hold values from -6 to 6
- block_mask: int32 [32, 112], replicated, may hold values from 0 to 1, as said below
- gate_blocks: bfloat16 [2240, 128, 128], P('tensor'), may hold values from -0.125 to 0.125
- up_blocks: bfloat16 [2240, 128, 128], P('tensor'), may hold values from -0.125 to 0.125
- down_blocks: bfloat16 [2240, 128, 128], P('tensor'), may hold values from -0.0625 to 0.0625
Outputs:
- mixed: bfloat16 [1280, 4096], P(('dp', 'tensor'))
- grad_tokens: bfloat16 [1280, 4096], P(('dp', 'tensor'))
- grad_gate: bfloat16 [2240, 128, 128], P('tensor', 'dp')
- grad_up: bfloat16 [2240, 128, 128], P('tensor', 'dp')
- grad_down: bfloat16 [2240, 128, 128], P('tensor', 'dp')
Inputs may be any that keep to these rules, and one draw needn't show every extreme that they name: `block_mask`: each shard of 7 consecutive hidden column blocks keeps at most 140 of its 224 blocks, and some shard keeps exactly 140; the same mask prunes all three projections.
All inputs are finite; a program needn't handle non-finite values.
Results may differ from a plain program's by a relative error of at most 0.023.
Values may be sent and summed in bfloat16 or wider, within the bound.
A program may use at most 192 MiB of HBM per device.

v0:
```python
import jax
import jax.numpy as jnp
from jax import lax
from jax.sharding import PartitionSpec as P


def on_device(tokens, grad_out, block_mask, gate_blocks, up_blocks, down_blocks):
    shard_count = lax.axis_size("tensor")
    shard_id = lax.axis_index("tensor")
    row_blocks = block_mask.shape[0]
    col_blocks = block_mask.shape[1] // shard_count
    block_size = gate_blocks.shape[1]
    capacity = gate_blocks.shape[0]
    local_mask = lax.dynamic_slice_in_dim(block_mask, shard_id * col_blocks, col_blocks, 1).reshape(
        -1
    )
    slot_index = jnp.nonzero(local_mask, size=capacity, fill_value=0)[0].astype(jnp.int32)
    slot_live = jnp.arange(capacity, dtype=jnp.int32) < jnp.sum(local_mask)
    block_rows = slot_index // col_blocks
    block_cols = slot_index % col_blocks
    row_onehot = (
        (block_rows[:, None] == jnp.arange(row_blocks, dtype=jnp.int32)[None, :])
        & slot_live[:, None]
    ).astype(jnp.float32)
    col_onehot = (
        (block_cols[:, None] == jnp.arange(col_blocks, dtype=jnp.int32)[None, :])
        & slot_live[:, None]
    ).astype(jnp.float32)

    def take_blocks(matrix, index, count):
        return jnp.take(matrix.reshape(matrix.shape[0], count, block_size), index, axis=1)

    def combine(parts, onehot):
        summed = jnp.einsum("gkn,kc->gcn", parts, onehot, precision=lax.Precision.HIGHEST)
        return summed.reshape(parts.shape[0], -1)

    def live_only(term):
        return jnp.where(slot_live[:, None, None], term, jnp.zeros_like(term))

    all_tokens = lax.all_gather(tokens, "tensor", axis=0, tiled=True)
    tok_parts = take_blocks(all_tokens, block_rows, row_blocks)
    gate_pre = combine(
        jnp.einsum("gkb,kbn->gkn", tok_parts, gate_blocks, preferred_element_type=jnp.float32),
        col_onehot,
    )
    up_pre = combine(
        jnp.einsum("gkb,kbn->gkn", tok_parts, up_blocks, preferred_element_type=jnp.float32),
        col_onehot,
    )
    sigmoid_gate = jax.nn.sigmoid(gate_pre)
    silu_gate = gate_pre * sigmoid_gate
    hidden = (silu_gate * up_pre).astype(jnp.bfloat16)
    hid_parts = take_blocks(hidden, block_cols, col_blocks)
    out_partial = combine(
        jnp.einsum("gkb,kbn->gkn", hid_parts, down_blocks, preferred_element_type=jnp.float32),
        row_onehot,
    )
    mixed = lax.psum_scatter(
        out_partial.astype(jnp.bfloat16), "tensor", scatter_dimension=0, tiled=True
    )
    all_grads = lax.all_gather(grad_out, "tensor", axis=0, tiled=True)
    cot_parts = take_blocks(all_grads, block_rows, row_blocks)
    grad_hidden = combine(
        jnp.einsum("gkn,kbn->gkb", cot_parts, down_blocks, preferred_element_type=jnp.float32),
        col_onehot,
    )
    grad_gate_act = (
        grad_hidden * up_pre * sigmoid_gate * (1.0 + gate_pre * (1.0 - sigmoid_gate))
    ).astype(jnp.bfloat16)
    grad_up_act = (grad_hidden * silu_gate).astype(jnp.bfloat16)
    down_term = live_only(
        jnp.einsum("gkb,gkn->kbn", hid_parts, cot_parts, preferred_element_type=jnp.float32)
    )
    gga_parts = take_blocks(grad_gate_act, block_cols, col_blocks)
    gua_parts = take_blocks(grad_up_act, block_cols, col_blocks)
    input_parts = jnp.einsum(
        "gkn,kbn->gkb", gga_parts, gate_blocks, preferred_element_type=jnp.float32
    ) + jnp.einsum("gkn,kbn->gkb", gua_parts, up_blocks, preferred_element_type=jnp.float32)
    input_partial = combine(input_parts, row_onehot)
    grad_tokens = lax.psum_scatter(
        input_partial.astype(jnp.bfloat16), "tensor", scatter_dimension=0, tiled=True
    )
    gate_term = live_only(
        jnp.einsum("gkb,gkn->kbn", tok_parts, gga_parts, preferred_element_type=jnp.float32)
    )
    up_term = live_only(
        jnp.einsum("gkb,gkn->kbn", tok_parts, gua_parts, preferred_element_type=jnp.float32)
    )
    gate_sum, up_sum, down_sum = (
        lax.psum_scatter(
            gate_term.astype(jnp.bfloat16), "dp", scatter_dimension=1, tiled=True
        ).astype(jnp.float32),
        lax.psum_scatter(
            up_term.astype(jnp.bfloat16), "dp", scatter_dimension=1, tiled=True
        ).astype(jnp.float32),
        lax.psum_scatter(
            down_term.astype(jnp.bfloat16), "dp", scatter_dimension=1, tiled=True
        ).astype(jnp.float32),
    )
    return (
        mixed,
        grad_tokens,
        gate_sum.astype(jnp.bfloat16),
        up_sum.astype(jnp.bfloat16),
        down_sum.astype(jnp.bfloat16),
    )


def solution(mesh):
    in_specs = (
        P(("dp", "tensor"), None),
        P(("dp", "tensor"), None),
        P(),
        P("tensor", None, None),
        P("tensor", None, None),
        P("tensor", None, None),
    )
    out_specs = (
        P(("dp", "tensor"), None),
        P(("dp", "tensor"), None),
        P("tensor", "dp", None),
        P("tensor", "dp", None),
        P("tensor", "dp", None),
    )
    return jax.shard_map(
        on_device, mesh=mesh, in_specs=in_specs, out_specs=out_specs, check_vma=False
    )
```

profile of v0, /device:TPU:0, one launch (start us, length us, event | category | flops | bytes accessed | tf_op | source)
XLA Modules:
  0.0 729.4 jit_solution(10305609933393660421)
XLA Ops:
  15.0 45.6 %all-gather.5.cloned.1.call-done = bf16[16,10,4096]{2,1,0:T(8,128)(2,1)} async-done(((bf16[1,10,4096]{2,1,0:T(8,128)(2,1)}), bf16[16,10,4096]{2,1,0:T(8,128)(2,1)}) %all-gather.5.cloned.1.call-update) | async-done | bytes 1310736 | tf_op jit(solution)/shard_map/all_gather | solution.py:40
  63.9 45.6 %all-gather.7.cloned.1.call-done = bf16[16,10,4096]{2,1,0:T(8,128)(2,1)} async-done(((bf16[1,10,4096]{2,1,0:T(8,128)(2,1)}), bf16[16,10,4096]{2,1,0:T(8,128)(2,1)}) %all-gather.7.cloned.1.call-update) | async-done | bytes 1310736 | tf_op jit(solution)/shard_map/all_gather | solution.py:61
  109.5 3.8 reshape.86
  115.1 8.3 %gather_fusion = bf16[140,160,128]{2,1,0:T(8,128)(2,1)} fusion(bf16[160,32,128]{2,0,1:T(8,128)(2,1)S(1)} %copy.29, s32[1024]{0:T(1024)S(1)} %pad_clamp_fusion.1), kind=kCustom, calls=%fused_computation.clone | custom fusion | bytes 11469360 | tf_op jit(solution)/shard_map/jit(_take)/gather | solution.py:31
  123.4 8.4 %gather_fusion.2 = bf16[140,160,128]{2,1,0:T(8,128)(2,1)} fusion(bf16[160,32,128]{2,0,1:T(8,128)(2,1)S(1)} %copy.35, s32[1024]{0:T(1024)S(1)} %pad_clamp_fusion.1), kind=kCustom, calls=%fused_computation.2.clone | custom fusion | bytes 11469360 | tf_op jit(solution)/shard_map/jit(_take)/gather | solution.py:31
  131.8 11.6 %fusion.40 = f32[160,140,128]{2,0,1:T(8,128)} fusion(bf16[140,128,128]{2,1,0:T(8,128)(2,1)} %param.15, bf16[140,160,128]{2,1,0:T(8,128)(2,1)} %gather_fusion.2, pred[140]{0:T(512)(128)(4,1)S(1)} %get-tuple-element.12), kind=kOutput, calls=%fused_computation.49 | convolution fusion | flops 736870400 | bytes 21790860 | tf_op jit(solution)/shard_map/gkn,kbn->gkb/dot_general | solution.py:64
  143.4 11.6 %fusion.2 = f32[7,160,128]{2,0,1:T(8,128)S(1)} fusion(f32[160,140,128]{2,0,1:T(8,128)} %fusion.40, s32[140]{0:T(256)S(1)} %get-tuple-element.10, pred[140]{0:T(512)(128)(4,1)S(1)} %iota_compare_fusion.2), kind=kOutput, calls=%fused_computation.8 | convolution fusion | flops 240846752 | bytes 12042940 | tf_op jit(solution)/shard_map/gkn,kc->gcn/dot_general | solution.py:34
  158.7 10.4 %fusion.6 = f32[7,160,128]{2,0,1:T(8,128)S(1)} fusion(f32[160,140,128]{2,0,1:T(8,128)S(1)} %fusion.34, s32[140]{0:T(256)S(1)} %get-tuple-element.10, pred[140]{0:T(512)(128)(4,1)S(1)} %iota_compare_fusion.2), kind=kOutput, calls=%fused_computation.12 | convolution fusion | flops 240846752 | bytes 12042940 | tf_op jit(solution)/shard_map/gkn,kc->gcn/dot_general | solution.py:34
  172.9 10.4 %fusion.8 = f32[7,160,128]{2,0,1:T(8,128)S(1)} fusion(f32[160,140,128]{2,0,1:T(8,128)S(1)} %fusion.31, s32[140]{0:T(256)S(1)} %get-tuple-element.10, pred[140]{0:T(512)(128)(4,1)S(1)} %iota_compare_fusion.2), kind=kOutput, calls=%fused_computation.14 | convolution fusion | flops 240846752 | bytes 12042940 | tf_op jit(solution)/shard_map/gkn,kc->gcn/dot_general | solution.py:34
  183.8 8.5 %gather_fusion.3 = bf16[140,160,128]{2,1,0:T(8,128)(2,1)} fusion(bf16[160,7,128]{2,0,1:T(8,128)(2,1)S(1)} %get-tuple-element.16, s32[1024]{0:T(1024)S(1)} %pad_clamp_fusion), kind=kCustom, calls=%fused_computation.3.clone | custom fusion | bytes 11469360 | tf_op jit(solution)/shard_map/jit(_take)/gather | solution.py:31
  192.3 8.2 %gather_fusion.1 = bf16[140,160,128]{2,1,0:T(8,128)(2,1)} fusion(bf16[160,7,128]{2,0,1:T(8,128)(2,1)S(1)} %get-tuple-element.17, s32[1024]{0:T(1024)S(1)} %pad_clamp_fusion), kind=kCustom, calls=%fused_computation.1.clone | custom fusion | bytes 11469360 | tf_op jit(solution)/shard_map/jit(_take)/gather | solution.py:31
  200.5 8.6 %gather_fusion.4 = bf16[140,160,128]{2,1,0:T(8,128)(2,1)} fusion(bf16[160,7,128]{2,0,1:T(8,128)(2,1)S(1)} %get-tuple-element.18, s32[1024]{0:T(1024)S(1)} %pad_clamp_fusion), kind=kCustom, calls=%fused_computation.4.clone | custom fusion | bytes 11469360 | tf_op jit(solution)/shard_map/jit(_take)/gather | solution.py:31
  209.1 11.5 %fusion.12 = f32[140,160,128]{2,1,0:T(8,128)} fusion(bf16[140,128,128]{2,1,0:T(8,128)(2,1)} %param.14, bf16[140,160,128]{2,1,0:T(8,128)(2,1)} %gather_fusion.4, pred[140]{0:T(512)(128)(4,1)S(1)} %get-tuple-element.9), kind=kOutput, calls=%fused_computation.22 | convolution fusion | flops 736870400 | bytes 21790860 | tf_op jit(solution)/shard_map/gkn,kbn->gkb/dot_general | solution.py:78
  220.6 14.8 %add_bitcast_fusion = f32[160,140,128]{2,0,1:T(8,128)} fusion(f32[140,160,128]{2,1,0:T(8,128)} %fusion.12, bf16[140,128,128]{2,1,0:T(8,128)(2,1)} %param.13, bf16[140,160,128]{2,1,0:T(8,128)(2,1)} %gather_fusion.3, pred[140]{0:T(512)(128)(4,1)S(1)} %get-tuple-element.9), kind=kOutput, calls=%fused_computation.16 | convolution fusion | flops 739737600 | bytes 33259660 | tf_op jit(solution)/shard_map/gkn,kbn->gkb/dot_general | solution.py:76
  235.3 14.5 %fusion.60 = bf16[32,160,128]{2,0,1:T(8,128)(2,1)S(1)} fusion(f32[160,140,128]{2,0,1:T(8,128)} %add_bitcast_fusion, s32[140]{0:T(256)S(1)} %get-tuple-element.13, pred[140]{0:T(512)(128)(4,1)S(1)} %iota_compare_fusion.2), kind=kOutput, calls=%fused_computation.51 | convolution fusion | flops 1101669120 | bytes 12780220 | tf_op jit(solution)/shard_map/gkn,kc->gcn/dot_general | solution.py:34
  251.5 5.7 fusion.37
  257.2 11.0 %fusion.57 = bf16[32,160,128]{2,0,1:T(8,128)(2,1)S(1)} fusion(f32[160,140,128]{2,0,1:T(8,128)S(1)} %fusion.37, s32[140]{0:T(256)S(1)} %get-tuple-element.13, pred[140]{0:T(512)(128)(4,1)S(1)} %iota_compare_fusion.2), kind=kOutput, calls=%fused_computation.50 | convolution fusion | flops 1101669120 | bytes 12780220 | tf_op jit(solution)/shard_map/gkn,kc->gcn/dot_general | solution.py:34
  269.9 10.2 %select_convert_fusion.2 = bf16[140,128,128]{2,1,0:T(8,128)(2,1)} fusion(pred[140]{0:T(512)(128)(4,1)S(1)} %iota_compare_fusion.2, bf16[140,160,128]{2,1,0:T(8,128)(2,1)} %gather_fusion.3, pred[140]{0:T(512)(128)(4,1)S(1)} %get-tuple-element.9, bf16[140,160,128]{2,1,0:T(8,128)(2,1)} %gather_fusion, pred[140]{0:T(512)(128)(4,1)S(1)} %get-tuple-element.12), kind=kOutput, calls=%fused_computation.19 | convolution fusion | flops 744325120 | bytes 16056740 | tf_op jit(solution)/shard_map/gkb,gkn->kbn/dot_general | solution.py:84
  280.4 10.2 %select_convert_fusion = bf16[140,128,128]{2,1,0:T(8,128)(2,1)} fusion(pred[140]{0:T(512)(128)(4,1)S(1)} %iota_compare_fusion.2, bf16[140,160,128]{2,1,0:T(8,128)(2,1)} %gather_fusion.2, pred[140]{0:T(512)(128)(4,1)S(1)} %get-tuple-element.12, bf16[140,160,128]{2,1,0:T(8,128)(2,1)} %gather_fusion.1, pred[140]{0:T(512)(128)(4,1)S(1)} %get-tuple-element.9), kind=kOutput, calls=%fused_computation.17 | convolution fusion | flops 744325120 | bytes 16056740 | tf_op jit(solution)/shard_map/gkb,gkn->kbn/dot_general | solution.py:72
  290.7 10.3 %select_convert_fusion.1 = bf16[140,128,128]{2,1,0:T(8,128)(2,1)} fusion(pred[140]{0:T(512)(128)(4,1)S(1)} %iota_compare_fusion.2, bf16[140,160,128]{2,1,0:T(8,128)(2,1)} %gather_fusion.4, pred[140]{0:T(512)(128)(4,1)S(1)} %get-tuple-element.9, bf16[140,160,128]{2,1,0:T(8,128)(2,1)} %gather_fusion, pred[140]{0:T(512)(128)(4,1)S(1)} %get-tuple-element.12), kind=kOutput, calls=%fused_computation.18 | convolution fusion | flops 744325120 | bytes 16056740 | tf_op jit(solution)/shard_map/gkb,gkn->kbn/dot_general | solution.py:87
  302.3 115.8 %all-reduce.7.cloned.1.call-done = (bf16[160,4096]{1,0:T(8,128)(2,1)}, bf16[160,4096]{1,0:T(8,128)(2,1)}) async-done(((bf16[160,4096]{1,0:T(8,128)(2,1)}, bf16[160,4096]{1,0:T(8,128)(2,1)}), (bf16[160,4096]{1,0:T(8,128)(2,1)}, bf16[160,4096]{1,0:T(8,128)(2,1)})) %all-reduce.7.cloned.1.call-update) | async-done | bytes 2621456
  419.8 99.2 %reduce-scatter.4.cloned.1.call-done = bf16[140,16,128]{2,1,0:T(8,128)(2,1)} async-done(((bf16[140,128,128]{2,1,0:T(8,128)(2,1)}), bf16[140,16,128]{2,1,0:T(8,128)(2,1)}) %reduce-scatter.4.cloned.1.call-update) | async-done | bytes 573456 | tf_op jit(solution)/shard_map/reduce_scatter | solution.py:90
  519.0 101.6 %reduce-scatter.8.cloned.1.call-done = bf16[140,16,128]{2,1,0:T(8,128)(2,1)} async-done(((bf16[140,128,128]{2,1,0:T(8,128)(2,1)}), bf16[140,16,128]{2,1,0:T(8,128)(2,1)}) %reduce-scatter.8.cloned.1.call-update) | async-done | bytes 573456 | tf_op jit(solution)/shard_map/reduce_scatter | solution.py:96
  620.6 101.5 %reduce-scatter.6.cloned.1.call-done = bf16[140,16,128]{2,1,0:T(8,128)(2,1)} async-done(((bf16[140,128,128]{2,1,0:T(8,128)(2,1)}), bf16[140,16,128]{2,1,0:T(8,128)(2,1)}) %reduce-scatter.6.cloned.1.call-update) | async-done | bytes 573456 | tf_op jit(solution)/shard_map/reduce_scatter | solution.py:93
  (53 shorter events, 26.9 us)
Async XLA Ops:
  7.2 53.4 %all-gather.5.cloned.1.call-start = ((), (), s32[]{:S(2)}) async-start(), calls=%async_computation.6 | async-start | bytes 2228224 | tf_op jit(solution)/shard_map/all_gather | solution.py:40
  7.9 101.6 %all-gather.7.cloned.1.call-start = ((), (), s32[]{:S(2)}) async-start(), calls=%async_computation.7 | async-start | bytes 2228224 | tf_op jit(solution)/shard_map/all_gather | solution.py:61
  8.6 409.4 %all-reduce.7.cloned.1.call-start = ((), (), s32[]{:S(2)}) async-start(), calls=%async_computation.8 | async-start | bytes 5242880
  123.4 31.6 %slice-start = ((s8[5734400]{0:T(1024)(128)(4,1)}), s8[1540096]{0:T(1024)(128)(4,1)S(1)}, s32[]{:S(2)}) async-start(s8[5734400]{0:T(1024)(128)(4,1)} %bitcast.135), calls=%async_computation.9 | async-start | bytes 3080192
  131.8 23.3 %slice-start.1 = ((s8[5734400]{0:T(1024)(128)(4,1)}), s8[4194304]{0:T(1024)(128)(4,1)S(1)}, s32[]{:S(2)}) async-start(s8[5734400]{0:T(1024)(128)(4,1)} %bitcast.135), calls=%async_computation.10 | async-start | bytes 8388608
  269.8 249.2 %reduce-scatter.4.cloned.1.call-start = ((), (), s32[]{:S(2)}) async-start(), calls=%async_computation.3 | async-start | bytes 5160960 | tf_op jit(solution)/shard_map/reduce_scatter | solution.py:90
  280.1 340.6 %reduce-scatter.8.cloned.1.call-start = ((), (), s32[]{:S(2)}) async-start(), calls=%async_computation.5 | async-start | bytes 5160960 | tf_op jit(solution)/shard_map/reduce_scatter | solution.py:96
  290.6 10.4 %copy-start = (u32[128]{0:T(128)S(1)}, u32[128]{0:T(128)}, u32[]{:S(2)}) copy-start(u32[128]{0:T(128)} %constant.94) | copy-start | bytes 1540
  290.7 431.5 %reduce-scatter.6.cloned.1.call-start = ((), (), s32[]{:S(2)}) async-start(), calls=%async_computation.4 | async-start | bytes 5160960 | tf_op jit(solution)/shard_map/reduce_scatter | solution.py:93
Sparse Core Ops, SparseCore 0:
  10.5 50.0 all-gather.4
  63.0 46.3 all-gather.6
  270.0 148.0 all-reduce.6
  420.9 98.0 reduce-scatter.3
  522.0 98.5 reduce-scatter.7
  623.5 98.5 reduce-scatter.5
where the time goes:
time: 739 us; the launch traced here: 729 us
  waiting for transfers between devices  511 us (69%)
  matrix products  140 us (19%)
  local copies, waits for them, and re-layouts  57.1 us (8%)
  between operations  15.4 us (2%)
    unnamed x7, waiting for transfers between devices  117 us
    reduce_scatter x1, waiting for transfers between devices, on_device(): lax.psum_scatter(down_term.astype(jnp.bfloat16), 'dp', scatter_dimension=...  102 us
    reduce_scatter x1, waiting for transfers between devices, on_device(): lax.psum_scatter(up_term.astype(jnp.bfloat16), 'dp', scatter_dimension=1,...  101 us
    reduce_scatter x1, waiting for transfers between devices, on_device(): lax.psum_scatter(gate_term.astype(jnp.bfloat16), 'dp', scatter_dimension=...  99.2 us
    dot_general x5, matrix products, combine(): jnp.einsum('gkn,kc->gcn', parts, onehot, precision=lax.Precision.HIGHEST)  57.9 us
    all_gather x1, waiting for transfers between devices, on_device(): all_tokens = lax.all_gather(tokens, 'tensor', axis=0, tiled=True)  45.6 us
    all_gather x1, waiting for transfers between devices, on_device(): all_grads = lax.all_gather(grad_out, 'tensor', axis=0, tiled=True)  45.6 us
    gather x5, local copies, waits for them, and re-layouts, take_blocks(): jnp.take(matrix.reshape(matrix.shape[0], count, block_size), index, axis=1)  42 us
  transfers between devices with their start and end apart: 6, of which 6 were waited for; matrix products, arithmetic and copies ran while one was open for 6% of the time, Pallas kernels for 0%

commit v1 on v0

v1 whole, which is shorter than its diff:
```python
import functools

import jax
import jax.numpy as jnp
from jax import lax
from jax.experimental import pallas as pl
from jax.experimental.pallas import tpu as pltpu
from jax.sharding import PartitionSpec as P

MESH = pl.DeviceIdType.MESH
BF = jnp.bfloat16
F32 = jnp.float32


def nt_dot(a, b):
    return lax.dot_general(a, b, (((1,), (1,)), ((), ())), preferred_element_type=F32)


def tn_dot(a, b):
    return lax.dot_general(a, b, (((0,), (0,)), ((), ())), preferred_element_type=F32)


def kernel(
    dims,
    tok_ref, go_ref, slot_ref, kept_ref, gate_hbm, up_hbm, down_hbm,
    mixed_ref, gtok_ref, ggate_ref, gup_ref, gdown_ref,
    stage0, stage1, wgu, wd, chunks, rows, acts, hid, ggu, part, recv, cols, tokt,
    gblk, ublk, dblk, dsend, drecv, perm,
    load_sem, ag_send, ag_recv, fw_send,
    col_send, col_recv, colx_send, colx_recv,
    act_send, act_recv, rs_send, rs_recv, dn_send, dn_recv, loc_sem,
):
    ndp, nt, m, nh, rb, cb, cap = dims
    group = m * nt
    width = nh * 2048
    ds = width // ndp
    nchip = nt // 2
    rpd = rb // ndp
    d = lax.axis_index("dp")
    s = lax.axis_index("tensor")
    y, x = d // 2, d % 2
    chip, core = s // 2, s % 2
    ny = ndp // 2

    def peer(dd, ss):
        return (dd, ss)

    def rdma(src, dst, ssem, rsem, dev):
        return pltpu.make_async_remote_copy(
            src_ref=src, dst_ref=dst, send_sem=ssem, recv_sem=rsem,
            device_id=dev, device_id_type=MESH,
        )

    sib = chip * 2 + (1 - core)
    xp = y * 2 + (1 - x)
    yp = lax.rem(y + 1, ny) * 2 + x
    ym = lax.rem(y + ny - 1, ny) * 2 + x
    yp_o = lax.rem(y + 1, ny) * 2 + (1 - x)
    ym_o = lax.rem(y + ny - 1, ny) * 2 + (1 - x)
    y2 = lax.rem(y + 2, ny) * 2 + x
    y2_o = lax.rem(y + 2, ny) * 2 + (1 - x)

    load_g = pltpu.make_async_copy(gate_hbm, stage0.at[pl.ds(0, cap)], load_sem.at[0])
    load_u = pltpu.make_async_copy(up_hbm, stage1.at[pl.ds(0, cap)], load_sem.at[1])
    load_d = pltpu.make_async_copy(down_hbm, stage0.at[pl.ds(0, cap)], load_sem.at[2])
    barrier = pltpu.get_barrier_semaphore()
    for k in range(1, nt):
        pl.semaphore_signal(barrier, inc=1, device_id=peer(d, lax.rem(s + k, nt)), device_id_type=MESH)
    for k in range(1, ndp):
        pl.semaphore_signal(barrier, inc=1, device_id=peer(lax.rem(d + k, ndp), s), device_id_type=MESH)
    load_g.start()
    load_u.start()
    chunks[0, pl.ds(s * m, m)] = tok_ref[...]
    chunks[1, pl.ds(s * m, m)] = go_ref[...]
    stage0[cap] = jnp.zeros((128, 128), BF)
    stage1[cap] = jnp.zeros((128, 128), BF)
    ri = lax.broadcasted_iota(jnp.int32, (256, 256), 0)
    ci = lax.broadcasted_iota(jnp.int32, (256, 256), 1)
    perm[...] = jnp.where((ri // 16 == ci % 16) & (ri % 16 == ci // 16), 1.0, 0.0).astype(BF)
    pl.semaphore_wait(barrier, nt - 1 + ndp - 1)

    def chunk(src):
        return chunks.at[:, pl.ds(src * m, m)]

    def ag_copy(k):
        dst = lax.rem(chip + k, nchip) * 2 + core
        return rdma(chunk(s), chunk(s), ag_send.at[k], ag_recv.at[s], peer(d, dst))

    def fw_copy(k):
        src = lax.rem(chip + nchip - k, nchip) * 2 + core
        return rdma(chunk(src), chunk(src), fw_send.at[k], ag_recv.at[src], peer(d, sib))

    def ag_arrived(src):
        return rdma(chunk(src), chunk(src), ag_send.at[0], ag_recv.at[src], peer(d, sib))

    for k in range(1, nchip):
        ag_copy(k).start()
    fw_copy(0).start()

    def lay_inward(stage, lo):
        @pl.loop(0, rb)
        def _(r):
            for c in range(cb):
                blk = stage[slot_ref[r * cb + c]]
                for o in range(ndp):
                    wgu[c, pl.ds(pl.multiple_of(o * ds + r * 16, 16), 16), lo:lo + 128] = blk[o * 16:(o + 1) * 16]

    load_g.wait()
    lay_inward(stage0, 0)
    load_d.start()
    load_u.wait()
    lay_inward(stage1, 128)

    for k in range(1, nchip):
        ag_arrived(lax.rem(chip + nchip - k, nchip) * 2 + core).wait_recv()
        fw_copy(k).start()

    load_d.wait()

    @pl.loop(0, rb)
    def _(r):
        for c in range(cb):
            wd[c * 128:(c + 1) * 128, pl.ds(pl.multiple_of(r * 128, 128), 128)] = stage0[slot_ref[r * cb + c]]

    for k in range(nchip):
        ag_arrived(lax.rem(chip + nchip - k, nchip) * 2 + (1 - core)).wait_recv()

    pmat = perm[...]
    for a in range(2):
        @pl.loop(0, group // 16)
        def _(tb):
            t0 = pl.multiple_of(tb * 16, 16)
            for h in range(nh):
                mat = chunks[a, pl.ds(t0, 16), h].reshape(256, 128)
                out = jnp.dot(pmat, mat, preferred_element_type=F32).astype(BF)
                for j in range(16):
                    lo = (h * 16 + j) * 128
                    rows[a, pl.ds(t0, 16), lo:lo + 128] = out[j * 16:(j + 1) * 16]

    def col_slice(o):
        return rows.at[core, :, pl.ds(pl.multiple_of(o * ds, 128), ds)]

    def col_copy(k):
        dst = lax.rem(d + k, ndp)
        return rdma(col_slice(dst), cols.at[core, d], col_send.at[k], col_recv.at[d], peer(dst, s))

    def col_arrived(src):
        return rdma(cols.at[core, src], cols.at[core, src], col_send.at[0], col_recv.at[src], peer(d, sib))

    for k in range(1, ndp):
        col_copy(k).start()
    own_cols = pltpu.make_async_copy(col_slice(d), cols.at[core, d], loc_sem.at[0])
    own_cols.start()

    def act_copy(c, g, n, dst):
        return rdma(acts.at[c, g], acts.at[c, g], act_send.at[c, n], act_recv.at[c, g], peer(dst, s))

    def act_arrived(c, g):
        act_copy(c, g, 0, xp).wait_recv()

    @pl.loop(0, cb)
    def _(c):
        gu = jnp.dot(rows[0], wgu[c], preferred_element_type=F32)
        gh = nt_dot(rows[1], wd[pl.ds(pl.multiple_of(c * 128, 128), 128), :])
        gate, up = gu[:, :128], gu[:, 128:]
        sig = jax.nn.sigmoid(gate)
        silu = gate * sig
        hidden = (silu * up).astype(BF)
        gga = (gh * up * sig * (1.0 + gate * (1.0 - sig))).astype(BF)
        gua = (gh * silu).astype(BF)
        acts[c, d, :, 0:128] = gga
        acts[c, d, :, 128:256] = gua
        acts[c, d, :, 256:384] = hidden
        act_copy(c, d, 0, xp).start()
        act_copy(c, d, 1, yp).start()
        act_copy(c, d, 2, ym).start()
        ggu[:, pl.ds(pl.multiple_of(c * 256, 128), 128)] = gga
        ggu[:, pl.ds(pl.multiple_of(c * 256 + 128, 128), 128)] = gua
        hid[:, pl.ds(pl.multiple_of(c * 128, 128), 128)] = hidden

    for k in range(1, nchip):
        ag_copy(k).wait_send()
    for k in range(nchip):
        fw_copy(k).wait_send()

    @pl.loop(0, cb)
    def _(c):
        act_arrived(c, xp)
        act_copy(c, xp, 3, yp).start()
        act_copy(c, xp, 4, ym).start()

    step = min(512, width)

    @pl.loop(0, width // step)
    def _(n):
        lo = pl.multiple_of(n * step, step)
        part[0, :, pl.ds(lo, step)] = jnp.dot(
            hid[...], wd[:, pl.ds(lo, step)], preferred_element_type=F32
        ).astype(BF)
        wide = jnp.concatenate([wgu[c, pl.ds(lo, step), :] for c in range(cb)], axis=1)
        part[1, :, pl.ds(lo, step)] = nt_dot(ggu[...], wide).astype(BF)

    for a in range(2):
        @pl.loop(0, group // 16)
        def _(tb):
            t0 = pl.multiple_of(tb * 16, 16)
            for h in range(nh):
                mat = jnp.concatenate(
                    [part[a, pl.ds(t0, 16), (h * 16 + j) * 128:(h * 16 + j + 1) * 128] for j in range(16)],
                    axis=0,
                )
                out = jnp.dot(pmat, mat, preferred_element_type=F32).astype(BF)
                chunks[a, pl.ds(t0, 16), h] = out.reshape(16, 16, 128)

    def rs_copy(k):
        dst = lax.rem(s + k, nt)
        return rdma(chunk(dst), recv.at[:, s], rs_send.at[k], rs_recv.at[s], peer(d, dst))

    for k in range(1, nt):
        rs_copy(k).start()
    for a in range(2):
        recv[a, s] = chunks[a, pl.ds(s * m, m)]

    @pl.loop(0, cb)
    def _(c):
        act_arrived(c, ym)
        act_copy(c, ym, 5, yp).start()
        act_arrived(c, yp_o)
        act_copy(c, yp_o, 6, ym).start()

    own_cols.wait()
    for k in range(1, ndp):
        col_arrived(lax.rem(d + k, ndp)).wait_recv()
    colx = rdma(cols.at[core], cols.at[core], colx_send, colx_recv, peer(d, sib))
    colx.start()
    rdma(cols.at[1 - core], cols.at[1 - core], colx_send, colx_recv, peer(d, sib)).wait_recv()
    total = ndp * group
    tall = cols[0].reshape(total, ds)
    for q in range(total // 128):
        tokt[:, q * 128:(q + 1) * 128] = tall[q * 128:(q + 1) * 128].T

    def dn_copy(c, k):
        dst = lax.rem(d + k, ndp)
        return rdma(dsend.at[dst, c], drecv.at[d, c], dn_send.at[k], dn_recv.at[d], peer(dst, s))

    @pl.loop(0, cb)
    def _(c):
        for g in (ym_o, yp, y2, y2_o):
            act_arrived(c, g)
        down = tn_dot(acts[c, :, :, 256:384].reshape(total, 128), cols[1].reshape(total, ds)).astype(BF)
        for o in range(ndp):
            dsend[o, c] = down[o * 16:(o + 1) * 16]
        for k in range(1, ndp):
            dn_copy(c, k).start()
        drecv[d, c] = dsend[d, c]
        both = jnp.dot(
            tokt[...], acts[c, :, :, 0:256].reshape(total, 256), preferred_element_type=F32
        ).astype(BF)
        for r in range(rb):
            gblk[r * cb + c] = both[r * 16:(r + 1) * 16, :128]
            ublk[r * cb + c] = both[r * 16:(r + 1) * 16, 128:]

    zero = jnp.zeros((16, 128), BF)
    gblk[rb * cb] = zero
    ublk[rb * cb] = zero
    dblk[rb * cb] = zero

    @pl.loop(0, cap)
    def _(k):
        ggate_ref[k] = gblk[kept_ref[k]]
        gup_ref[k] = ublk[kept_ref[k]]

    for k in range(1, nt):
        src = lax.rem(s + k, nt)
        rdma(recv.at[:, src], recv.at[:, src], rs_send.at[0], rs_recv.at[src], peer(d, sib)).wait_recv()

    @pl.loop(0, m)
    def _(t):
        mixed_ref[t] = jnp.sum(recv[0, :, t].astype(F32), axis=0).astype(BF)
        gtok_ref[t] = jnp.sum(recv[1, :, t].astype(F32), axis=0).astype(BF)

    for k in range(1, ndp):
        src = lax.rem(d + k, ndp)
        rdma(drecv.at[src], drecv.at[src], dn_send.at[0], dn_recv.at[src], peer(d, sib)).wait_recv()
    for r in range(rb):
        for c in range(cb):
            lo = (r % rpd) * 128
            dblk[r * cb + c] = drecv[r // rpd, c, :, lo:lo + 128]

    @pl.loop(0, cap)
    def _(k):
        gdown_ref[k] = dblk[kept_ref[k]]

    for k in range(1, ndp):
        col_copy(k).wait_send()
        rdma(dsend.at[lax.rem(d + k, ndp)], drecv.at[d], dn_send.at[k], dn_recv.at[d], peer(d, sib)).wait_send()
    colx.wait_send()
    for k in range(1, nt):
        rs_copy(k).wait_send()

    @pl.loop(0, cb)
    def _(c):
        for n, g in enumerate((d, d, d, xp, xp, ym, yp_o)):
            act_copy(c, g, n, xp).wait_send()


def on_device(tokens, grad_out, block_mask, gate_blocks, up_blocks, down_blocks):
    nt = lax.axis_size("tensor")
    ndp = lax.axis_size("dp")
    shard = lax.axis_index("tensor")
    rb = block_mask.shape[0]
    cb = block_mask.shape[1] // nt
    cap = gate_blocks.shape[0]
    m, width = tokens.shape
    nh = width // 2048
    group = m * nt
    ds = width // ndp
    nb = rb * cb
    flags = lax.dynamic_slice_in_dim(block_mask, shard * cb, cb, 1).reshape(-1)
    pos = jnp.arange(nb, dtype=jnp.int32)
    upto = jnp.sum(jnp.where(pos[None, :] <= pos[:, None], flags[None, :], 0), axis=1)
    slot = jnp.where(flags > 0, upto - 1, cap)
    kept = jnp.sum((upto[None, :] <= jnp.arange(cap, dtype=jnp.int32)[:, None]).astype(jnp.int32), axis=1)

    tok = tokens.reshape(m, rb, ndp, 16).transpose(0, 2, 1, 3).reshape(m, nh, 16, 128)
    go = grad_out.reshape(m, nh, 16, 128)

    vm = pl.BlockSpec(memory_space=pltpu.VMEM)
    sm = pl.BlockSpec(memory_space=pltpu.SMEM)
    hb = pl.BlockSpec(memory_space=pl.ANY)
    dma = pltpu.SemaphoreType.DMA
    row_chunk = jax.ShapeDtypeStruct((m, nh, 16, 128), BF)
    grad = jax.ShapeDtypeStruct((cap, 16, 128), BF)
    mixed, gtok, ggate, gup, gdown = pl.pallas_call(
        functools.partial(kernel, (ndp, nt, m, nh, rb, cb, cap)),
        out_shape=(row_chunk, row_chunk, grad, grad, grad),
        in_specs=[vm, vm, sm, sm, hb, hb, hb],
        out_specs=[vm] * 5,
        scratch_shapes=[
            pltpu.VMEM((cap + 1, 128, 128), BF),
            pltpu.VMEM((cap + 1, 128, 128), BF),
            pltpu.VMEM((cb, width, 256), BF),
            pltpu.VMEM((cb * 128, width), BF),
            pltpu.VMEM((2, group, nh, 16, 128), BF),
            pltpu.VMEM((2, group, width), BF),
            pltpu.VMEM((cb, ndp, group, 384), BF),
            pltpu.VMEM((group, cb * 128), BF),
            pltpu.VMEM((group, cb * 256), BF),
            pltpu.VMEM((2, group, width), BF),
            pltpu.VMEM((2, nt, m, nh, 16, 128), BF),
            pltpu.VMEM((2, ndp, group, ds), BF),
            pltpu.VMEM((ds, ndp * group), BF),
            pltpu.VMEM((nb + 1, 16, 128), BF),
            pltpu.VMEM((nb + 1, 16, 128), BF),
            pltpu.VMEM((nb + 1, 16, 128), BF),
            pltpu.VMEM((ndp, cb, 16, ds), BF),
            pltpu.VMEM((ndp, cb, 16, ds), BF),
            pltpu.VMEM((256, 256), BF),
            dma((3,)),
            dma((nt,)),
            dma((nt,)),
            dma((nt,)),
            dma((ndp,)),
            dma((ndp,)),
            dma,
            dma,
            dma((cb, 7)),
            dma((cb, ndp)),
            dma((nt,)),
            dma((nt,)),
            dma((ndp,)),
            dma((ndp,)),
            dma((1,)),
        ],
        compiler_params=pltpu.CompilerParams(
            collective_id=0, has_side_effects=True, vmem_limit_bytes=64 * 1024 * 1024
        ),
    )(tok, go, slot, kept, gate_blocks, up_blocks, down_blocks)
    grad_tokens = gtok.reshape(m, ndp, rb, 16).transpose(0, 2, 1, 3).reshape(m, width)
    return mixed.reshape(m, width), grad_tokens, ggate, gup, gdown


def solution(mesh):
    rows = P(("dp", "tensor"), None)
    blocks = P("tensor", None, None)
    grads = P("tensor", "dp", None)
    return jax.shard_map(
        on_device,
        mesh=mesh,
        in_specs=(rows, rows, P(), blocks, blocks, blocks),
        out_specs=(rows, rows, grads, grads, grads),
        check_vma=False,
    )
```

time: 739 us -> 140 us (0.19); the launches traced: 729 us -> 139 us
  waiting for transfers between devices: 511 us -> 0 us
  matrix products: 140 us -> 0 us
  Pallas kernels: 0 us -> 124 us
  local copies, waits for them, and re-layouts: 57.1 us -> 13.5 us
  between operations: 15.4 us -> 0.71 us
    reduce_scatter x3 -> x0, waiting for transfers between devices: 302 us -> none  [the longest x1 102 us: on_device(): lax.psum_scatter(down_term.astype(jnp.bfloat16), 'dp', scatter_dimension=...]
    dot_general x14 -> x0, matrix products: 140 us -> none  [the longest x5 57.9 us: combine(): jnp.einsum('gkn,kc->gcn', parts, onehot, precision=lax.Precision.HIGHEST)]
    pallas_call x0 -> x1, Pallas kernels: none -> 124 us  [on_device(): pl.pallas_call(functools.partial(kernel, (ndp, nt, m, nh, rb, cb, cap)),...]
    unnamed x7 -> x0, waiting for transfers between devices: 117 us -> none
    all_gather x2 -> x0, waiting for transfers between devices: 91.1 us -> none  [the longest x1 45.6 us: on_device(): all_tokens = lax.all_gather(tokens, 'tensor', axis=0, tiled=True)]
    gather x5 -> x0, local copies, waits for them, and re-layouts: 42 us -> none  [take_blocks(): jnp.take(matrix.reshape(matrix.shape[0], count, block_size), index, axis=1)]
  transfers between devices with their start and end apart: 6 -> 0, of which waited for: 6 -> 0; matrix products, arithmetic and copies ran while one was open for 6% -> 0% of each run, Pallas kernels for 0% -> 0%
where the time goes in v1:
time: 140 us; the launch traced here: 139 us
  Pallas kernels  124 us (89%)
  local copies, waits for them, and re-layouts  13.5 us (10%)
    pallas_call x1, Pallas kernels, on_device(): pl.pallas_call(functools.partial(kernel, (ndp, nt, m, nh, rb, cb, cap)),...  124 us
    unnamed x11, local copies, waits for them, and re-layouts  6.77 us
    reshape x2, local copies, waits for them, and re-layouts, on_device(): gtok.reshape(m, ndp, rb, 16).transpose(0, 2, 1, 3).reshape(m, width)  2.98 us

profile of v1, /device:TPU:0, one launch (start us, length us, event | category | flops | bytes accessed | tf_op | source)
XLA Modules:
  0.0 139.2 jit_solution(168274531466436543)
XLA Ops:
  0.6 0.8 constant_dynamic-slice_fusion
  1.4 0.1 reshape.36
  1.5 0.1 select_reduce_fusion
  1.7 0.6 compare_select_fusion.slot_ref
  2.2 0.7 convert_reduce_fusion.kept_ref
  2.9 1.4 %reshape.33 = bf16[10,32,8,16]{3,2,1,0:T(8,128)(2,1)S(1)} reshape(bf16[10,4096]{1,0:T(8,128)(2,1)} %param.6) | data formatting | bytes 163840 | tf_op jit(solution)/shard_map/reshape | solution.py:325
  4.3 0.1 copy.15
  4.5 1.1 reshape.34.tok_ref
  5.5 0.9 copy.17
  6.4 0.6 slice
  7.1 123.6 %shard_map.101 = (bf16[10,2,16,128]{3,2,1,0:T(8,128)(2,1)}, bf16[10,2,16,128]{3,2,1,0:T(8,128)(2,1)}, bf16[140,16,128]{2,1,0:T(8,128)(2,1)}, bf16[140,16,128]{2,1,0:T(8,128)(2,1)}, bf16[140,16,128]{2,1,0:T(8,128)(2,1)}) custom-call(bf16[10,2,16,128]{3,2,1,0:T(8,128)(2,1)} %reshape.34.tok_ref, bf16[10,2,16,128]{3,2,1,0:T(8,128)(2,1)} %bitcast.20, ...), custom_call_target="tpu_custom_call" | custom-call | tf_op jit(solution)/shard_map/pallas_call | solution.py:334
  130.7 0.0 copy-start.1
  130.7 0.0 copy-start
  130.7 1.4 %reshape.38 = bf16[10,8,32,16]{3,2,1,0:T(8,128)(2,1)S(1)} reshape(bf16[10,2,16,128]{3,2,1,0:T(8,128)(2,1)} %get-tuple-element.11) | data formatting | bytes 163840 | tf_op jit(solution)/shard_map/reshape | solution.py:379
  132.1 0.3 copy.16
  132.4 1.6 %reshape.39 = bf16[10,4096]{1,0:T(8,128)(2,1)} reshape(bf16[10,32,8,16]{3,2,1,0:T(8,128)(2,1)S(1)} %copy.16) | data formatting | bytes 163840 | tf_op jit(solution)/shard_map/reshape | solution.py:379
  134.0 0.9 pad
  134.9 0.7 copy.18
  135.6 2.0 %copy.22 = bf16[140,16,128]{2,1,0:T(8,128)(2,1)} copy(bf16[140,16,128]{2,1,0:T(8,128)(2,1)} %get-tuple-element.22) | data formatting | bytes 1146880
  137.5 0.0 copy-done.1
  137.5 0.8 copy.23
  138.3 0.0 copy-done
  138.4 0.8 copy.24
Async XLA Ops:
  130.7 6.9 %copy-start.1 = (bf16[140,16,128]{2,1,0:T(8,128)(2,1)S(1)}, bf16[140,16,128]{2,1,0:T(8,128)(2,1)}, u32[]{:S(2)}) copy-start(bf16[140,16,128]{2,1,0:T(8,128)(2,1)} %get-tuple-element.23) | copy-start | bytes 1720324
  130.7 7.7 %copy-start = (bf16[140,16,128]{2,1,0:T(8,128)(2,1)S(1)}, bf16[140,16,128]{2,1,0:T(8,128)(2,1)}, u32[]{:S(2)}) copy-start(bf16[140,16,128]{2,1,0:T(8,128)(2,1)} %get-tuple-element.24) | copy-start | bytes 1720324

commit v2 on v1

v2 whole, which is shorter than its diff:
```python
import functools

import jax
import jax.numpy as jnp
from jax import lax
from jax.experimental import pallas as pl
from jax.experimental.pallas import tpu as pltpu
from jax.sharding import PartitionSpec as P

MESH = pl.DeviceIdType.MESH
BF = jnp.bfloat16
F32 = jnp.float32


def nt_dot(a, b):
    return lax.dot_general(a, b, (((1,), (1,)), ((), ())), preferred_element_type=F32)


def tn_dot(a, b):
    return lax.dot_general(a, b, (((0,), (0,)), ((), ())), preferred_element_type=F32)


def swap_matrix(outer, inner):
    n = outer * inner
    o = lax.broadcasted_iota(jnp.int32, (n, n), 0)
    i = lax.broadcasted_iota(jnp.int32, (n, n), 1)
    hit = (o // outer == i % inner) & (o % outer == i // inner)
    return jnp.where(hit, 1.0, 0.0).astype(BF)


def move(a, b):
    return jnp.dot(a, b, preferred_element_type=F32).astype(BF)


def kernel(
    dims,
    tok_ref, go_ref, slot_ref, kept_ref, gate_hbm, up_hbm, down_hbm,
    mixed_ref, gtok_ref, ggate_ref, gup_ref, gdown_ref,
    stage0, stage1, wgu, wd, own16, chunks, rows, gus, acth, actg, hid, ggu, sibx, recv, fin,
    qsend, qrecv, craw, cols, tokt, gblk, ublk, dblk, dsend, drecv, perm,
    load_sem, ag_send, ag_recv, fw_send, q_send, q_recv, cg_send, cg_recv, cf_send,
    h_send, h_recv, g_send, g_recv, sib_send, sib_recv, rs_send, rs_recv, dn_send, dn_recv,
):
    ndp, nt, m, nh, rb, cb, cap = dims
    group = m * nt
    width = nh * 2048
    ds = width // ndp
    nj = ds // 128
    nchip = nt // 2
    rpd = rb // ndp
    cm = m * 2 * nj // 16
    total = ndp * group
    d = lax.axis_index("dp")
    s = lax.axis_index("tensor")
    y, x = d // 2, d % 2
    chip, core = s // 2, s % 2
    ny = ndp // 2

    def rdma(src, dst, ssem, rsem, dev):
        return pltpu.make_async_remote_copy(
            src_ref=src, dst_ref=dst, send_sem=ssem, recv_sem=rsem,
            device_id=dev, device_id_type=MESH,
        )

    sib = chip * 2 + (1 - core)
    xp = y * 2 + (1 - x)
    yp = lax.rem(y + 1, ny) * 2 + x
    ym = lax.rem(y + ny - 1, ny) * 2 + x
    yp_o = lax.rem(y + 1, ny) * 2 + (1 - x)
    ym_o = lax.rem(y + ny - 1, ny) * 2 + (1 - x)
    y2 = lax.rem(y + 2, ny) * 2 + x
    y2_o = lax.rem(y + 2, ny) * 2 + (1 - x)

    def chip_ahead(k):
        return lax.rem(chip + k, nchip)

    def chip_behind(k):
        return lax.rem(chip + nchip - k, nchip)

    load_g = pltpu.make_async_copy(gate_hbm, stage0.at[pl.ds(0, cap)], load_sem.at[0])
    load_u = pltpu.make_async_copy(up_hbm, stage1.at[pl.ds(0, cap)], load_sem.at[1])
    load_d = pltpu.make_async_copy(down_hbm, stage0.at[pl.ds(0, cap)], load_sem.at[2])
    barrier = pltpu.get_barrier_semaphore()
    for k in range(1, nt):
        pl.semaphore_signal(barrier, inc=1, device_id=(d, lax.rem(s + k, nt)), device_id_type=MESH)
    for k in range(1, ndp):
        pl.semaphore_signal(barrier, inc=1, device_id=(lax.rem(d + k, ndp), s), device_id_type=MESH)
    load_g.start()
    load_u.start()
    stage0[cap] = jnp.zeros((128, 128), BF)
    stage1[cap] = jnp.zeros((128, 128), BF)
    own16[...] = jnp.zeros_like(own16)
    fin[...] = jnp.zeros_like(fin)
    own16[0, 0:m, :] = tok_ref[...]
    own16[1, 0:m, :] = go_ref[...]
    perm[...] = swap_matrix(16, 16)

    for a in range(2):
        mat = jnp.concatenate(
            [
                jnp.concatenate(
                    [own16[a, :, (h * 16 + j) * 128:(h * 16 + j + 1) * 128] for j in range(16)], axis=0
                )
                for h in range(nh)
            ],
            axis=1,
        )
        out = move(perm[...], mat)
        for h in range(nh):
            chunks[a, pl.ds(s * m, m), h] = out[:, h * 128:(h + 1) * 128].reshape(16, 16, 128)[:m]
    pl.semaphore_wait(barrier, nt - 1 + ndp - 1)

    def chunk(a, src):
        return chunks.at[a, pl.ds(src * m, m)]

    def ag_copy(a, k):
        dst = chip_ahead(k) * 2 + core
        return rdma(chunk(a, s), chunk(a, s), ag_send.at[a, k], ag_recv.at[a, s], (d, dst))

    def fw_copy(a, k):
        src = chip_behind(k) * 2 + core
        return rdma(chunk(a, src), chunk(a, src), fw_send.at[a, k], ag_recv.at[a, src], (d, sib))

    def ag_arrived(a, src):
        rdma(chunk(a, src), chunk(a, src), ag_send.at[a, 0], ag_recv.at[a, src], (d, sib)).wait_recv()

    for a in range(2):
        for k in range(1, nchip):
            ag_copy(a, k).start()
        fw_copy(a, 0).start()

    def lay_inward(stage, lo):
        @pl.loop(0, rb)
        def _(r):
            for c in range(cb):
                wgu[c, pl.ds(pl.multiple_of(r * 128, 128), 128), lo:lo + 128] = stage[slot_ref[r * cb + c]]

    load_g.wait()
    lay_inward(stage0, 0)
    load_d.start()
    load_u.wait()
    lay_inward(stage1, 128)

    @pl.loop(0, ndp // 2)
    def _(pair):
        stack = jnp.concatenate(
            [own16[0, :, q * 1024:(q + 1) * 1024] for q in range(width // 1024)], axis=0
        )
        i = lax.broadcasted_iota(jnp.int32, (1024, 256), 0)
        o = lax.broadcasted_iota(jnp.int32, (1024, 256), 1) + pair * 256
        hit = (i // 128 == (o // 16) % 8) & ((i // 16) % 8 == o // 128) & (i % 16 == o % 16)
        toks = move(stack, jnp.where(hit, 1.0, 0.0).astype(BF))
        halves = []
        for w in range(2):
            base = pl.multiple_of((pair * 2 + w) * ds, 128)
            gos = jnp.concatenate(
                [own16[1, :, pl.ds(pl.multiple_of(base + j * 128, 128), 128)] for j in range(nj)], axis=0
            )
            halves.append(jnp.concatenate([toks[:, w * 128:(w + 1) * 128], gos], axis=0))
        out = move(swap_matrix(2 * nj, 16), jnp.concatenate(halves, axis=1))
        for w in range(2):
            qsend[pair * 2 + w] = out[0:cm * 16, w * 128:(w + 1) * 128].reshape(cm, 16, 128)

    def q_copy(k):
        dst = lax.rem(d + k, ndp)
        return rdma(qsend.at[dst], qrecv.at[d], q_send.at[k], q_recv.at[d], (dst, s))

    for k in range(1, ndp):
        q_copy(k).start()
    qrecv[d] = qsend[d]

    def forward(a):
        for k in range(1, nchip):
            ag_arrived(a, chip_behind(k) * 2 + core)
            fw_copy(a, k).start()

    def to_rows(a):
        @pl.loop(0, group // 16)
        def _(tb):
            t0 = pl.multiple_of(tb * 16, 16)
            mat = jnp.concatenate(
                [chunks[a, pl.ds(t0, 16), h].reshape(256, 128) for h in range(nh)], axis=1
            )
            out = move(perm[...], mat)
            for h in range(nh):
                for j in range(16):
                    lo = (h * 16 + j) * 128
                    rows[a, pl.ds(t0, 16), lo:lo + 128] = out[j * 16:(j + 1) * 16, h * 128:(h + 1) * 128]

    forward(0)
    for k in range(nchip):
        ag_arrived(0, chip_behind(k) * 2 + (1 - core))
    to_rows(0)

    def h_copy(c, g, n, dst):
        return rdma(acth.at[c, g], acth.at[c, g], h_send.at[c, n], h_recv.at[c, g], (dst, s))

    def g_copy(c, g, n, dst):
        return rdma(actg.at[c, g], actg.at[c, g], g_send.at[c, n], g_recv.at[c, g], (dst, s))

    @pl.loop(0, cb)
    def _(c):
        gu = jnp.dot(rows[0], wgu[c], preferred_element_type=F32)
        gus[c] = gu
        gate, up = gu[:, :128], gu[:, 128:]
        hidden = (gate * jax.nn.sigmoid(gate) * up).astype(BF)
        acth[c, d] = hidden
        h_copy(c, d, 0, xp).start()
        h_copy(c, d, 1, yp).start()
        h_copy(c, d, 2, ym).start()
        hid[:, pl.ds(pl.multiple_of(c * 128, 128), 128)] = hidden

    forward(1)
    load_d.wait()

    @pl.loop(0, rb)
    def _(r):
        for c in range(cb):
            wd[c * 128:(c + 1) * 128, pl.ds(pl.multiple_of(r * 128, 128), 128)] = stage0[slot_ref[r * cb + c]]

    for k in range(nchip):
        ag_arrived(1, chip_behind(k) * 2 + (1 - core))
    to_rows(1)

    @pl.loop(0, cb)
    def _(c):
        gh = nt_dot(rows[1], wd[pl.ds(pl.multiple_of(c * 128, 128), 128), :])
        gu = gus[c]
        gate, up = gu[:, :128], gu[:, 128:]
        sig = jax.nn.sigmoid(gate)
        gga = (gh * up * sig * (1.0 + gate * (1.0 - sig))).astype(BF)
        gua = (gh * (gate * sig)).astype(BF)
        actg[c, d, :, 0:128] = gga
        actg[c, d, :, 128:256] = gua
        g_copy(c, d, 0, xp).start()
        g_copy(c, d, 1, yp).start()
        g_copy(c, d, 2, ym).start()
        ggu[:, pl.ds(pl.multiple_of(c * 256, 128), 128)] = gga
        ggu[:, pl.ds(pl.multiple_of(c * 256 + 128, 128), 128)] = gua

    @pl.loop(0, cb)
    def _(c):
        h_copy(c, xp, 0, xp).wait_recv()
        h_copy(c, xp, 3, yp).start()
        h_copy(c, xp, 4, ym).start()
        h_copy(c, ym, 0, xp).wait_recv()
        h_copy(c, ym, 5, yp).start()

    for k in range(1, ndp):
        src = lax.rem(d + k, ndp)
        rdma(qrecv.at[src], qrecv.at[src], q_send.at[0], q_recv.at[src], (d, sib)).wait_recv()

    def craw_of(src):
        return craw.at[:, pl.ds(src * cm, cm)]

    def cg_copy(k):
        dst = chip_ahead(k) * 2 + core
        return rdma(qrecv, craw_of(s), cg_send.at[k], cg_recv.at[s], (d, dst))

    own_to_sib = rdma(qrecv, craw_of(s), cg_send.at[0], cg_recv.at[s], (d, sib))

    def cf_copy(k):
        src = chip_behind(k) * 2 + core
        return rdma(craw_of(src), craw_of(src), cf_send.at[k], cg_recv.at[src], (d, sib))

    def cg_arrived(src):
        rdma(craw_of(src), craw_of(src), cg_send.at[0], cg_recv.at[src], (d, sib)).wait_recv()

    for k in range(1, nchip):
        cg_copy(k).start()
    own_to_sib.start()
    for g in range(ndp):
        craw[g, pl.ds(s * cm, cm)] = qrecv[g]

    for a in range(2):
        for k in range(1, nchip):
            ag_copy(a, k).wait_send()
        for k in range(nchip):
            fw_copy(a, k).wait_send()
    step = min(512, width)

    def to_chunks(a):
        @pl.loop(0, group // 16)
        def _(tb):
            t0 = pl.multiple_of(tb * 16, 16)
            mat = jnp.concatenate(
                [
                    jnp.concatenate(
                        [
                            rows[a, pl.ds(t0, 16), (h * 16 + j) * 128:(h * 16 + j + 1) * 128]
                            for j in range(16)
                        ],
                        axis=0,
                    )
                    for h in range(nh)
                ],
                axis=1,
            )
            out = move(perm[...], mat)
            for h in range(nh):
                chunks[a, pl.ds(t0, 16), h] = out[:, h * 128:(h + 1) * 128].reshape(16, 16, 128)

    def sib_copy(a, q):
        return rdma(chunk(a, q * 2 + (1 - core)), sibx.at[a, q], sib_send.at[a, q], sib_recv.at[a, q], (d, sib))

    @pl.loop(0, width // step)
    def _(n):
        lo = pl.multiple_of(n * step, step)
        rows[0, :, pl.ds(lo, step)] = jnp.dot(
            hid[...], wd[:, pl.ds(lo, step)], preferred_element_type=F32
        ).astype(BF)

    to_chunks(0)
    for q in range(nchip):
        sib_copy(0, q).start()

    @pl.loop(0, width // step)
    def _(n):
        lo = pl.multiple_of(n * step, step)
        wide = jnp.concatenate([wgu[c, pl.ds(lo, step), :] for c in range(cb)], axis=1)
        rows[1, :, pl.ds(lo, step)] = nt_dot(ggu[...], wide).astype(BF)

    to_chunks(1)
    for q in range(nchip):
        sib_copy(1, q).start()

    @pl.loop(0, cb)
    def _(c):
        g_copy(c, xp, 0, xp).wait_recv()
        g_copy(c, xp, 3, yp).start()
        g_copy(c, xp, 4, ym).start()
        g_copy(c, ym, 0, xp).wait_recv()
        g_copy(c, ym, 5, yp).start()

    def rs_copy(a, k):
        q = chip_ahead(k)
        return rdma(
            chunk(a, q * 2 + core), recv.at[a, chip], rs_send.at[a, k], rs_recv.at[a, chip], (d, q * 2 + core)
        )

    for a in range(2):
        for q in range(nchip):
            sib_copy(a, q).wait_recv()
        for k in range(nchip):
            q = chip_ahead(k)
            mine = pl.ds((q * 2 + core) * m, m)
            both = (chunks[a, mine].astype(F32) + sibx[a, q].astype(F32)).astype(BF)
            if k == 0:
                recv[a, chip] = both
            else:
                chunks[a, mine] = both
                rs_copy(a, k).start()

    @pl.loop(0, cb)
    def _(c):
        h_copy(c, yp_o, 0, xp).wait_recv()
        h_copy(c, yp_o, 6, ym).start()

    for k in range(1, nchip):
        cg_arrived(chip_behind(k) * 2 + core)
        cf_copy(k).start()
    for k in range(nchip):
        cg_arrived(chip_behind(k) * 2 + (1 - core))

    @pl.loop(0, ndp // 2)
    def _(gp):
        for tb in range(group // 32):
            per = 32 * 2 * nj // 16
            mat = jnp.concatenate(
                [craw[gp * 2 + w, tb * per:(tb + 1) * per].reshape(per * 16, 128) for w in range(2)], axis=1
            )
            out = move(swap_matrix(32, 2 * nj), mat)
            for w in range(2):
                for a in range(2):
                    for j in range(nj):
                        lo = (a * nj + j) * 32
                        cols[a, gp * 2 + w, tb * 32:(tb + 1) * 32, j * 128:(j + 1) * 128] = (
                            out[lo:lo + 32, w * 128:(w + 1) * 128]
                        )

    tall = cols[0].reshape(total, ds)
    for q in range(total // 128):
        tokt[:, q * 128:(q + 1) * 128] = tall[q * 128:(q + 1) * 128].T

    @pl.loop(0, cb)
    def _(c):
        g_copy(c, yp_o, 0, xp).wait_recv()
        g_copy(c, yp_o, 6, ym).start()

    def dn_copy(c, k):
        dst = lax.rem(d + k, ndp)
        return rdma(dsend.at[dst, c], drecv.at[d, c], dn_send.at[k], dn_recv.at[d], (dst, s))

    @pl.loop(0, cb)
    def _(c):
        for g in (ym_o, yp, y2, y2_o):
            h_copy(c, g, 0, xp).wait_recv()
        down = tn_dot(acth[c].reshape(total, 128), cols[1].reshape(total, ds)).astype(BF)
        for o in range(ndp):
            dsend[o, c] = down[o * 16:(o + 1) * 16]
        for k in range(1, ndp):
            dn_copy(c, k).start()
        drecv[d, c] = dsend[d, c]

    for a, out_ref in ((0, mixed_ref), (1, gtok_ref)):
        for k in range(1, nchip):
            q = chip_ahead(k)
            rdma(recv.at[a, q], recv.at[a, q], rs_send.at[a, 0], rs_recv.at[a, q], (d, sib)).wait_recv()
        fin[0:m] = jnp.sum(recv[a].astype(F32), axis=0).astype(BF)
        mat = jnp.concatenate([fin[:, h].reshape(256, 128) for h in range(nh)], axis=1)
        out = move(perm[...], mat)
        for h in range(nh):
            for j in range(16):
                lo = (h * 16 + j) * 128
                out_ref[:, lo:lo + 128] = out[j * 16:j * 16 + m, h * 128:(h + 1) * 128]

    @pl.loop(0, cb)
    def _(c):
        for g in (ym_o, yp, y2, y2_o):
            g_copy(c, g, 0, xp).wait_recv()
        both = jnp.dot(tokt[...], actg[c].reshape(total, 256), preferred_element_type=F32).astype(BF)
        for r in range(rb):
            gblk[r * cb + c] = both[r * 16:(r + 1) * 16, :128]
            ublk[r * cb + c] = both[r * 16:(r + 1) * 16, 128:]

    zero = jnp.zeros((16, 128), BF)
    gblk[rb * cb] = zero
    ublk[rb * cb] = zero
    dblk[rb * cb] = zero

    for k in range(1, ndp):
        src = lax.rem(d + k, ndp)
        rdma(drecv.at[src], drecv.at[src], dn_send.at[0], dn_recv.at[src], (d, sib)).wait_recv()
    for r in range(rb):
        for c in range(cb):
            lo = (r % rpd) * 128
            dblk[r * cb + c] = drecv[r // rpd, c, :, lo:lo + 128]

    @pl.loop(0, cap)
    def _(k):
        ggate_ref[k] = gblk[kept_ref[k]]
        gup_ref[k] = ublk[kept_ref[k]]
        gdown_ref[k] = dblk[kept_ref[k]]

    for k in range(1, ndp):
        q_copy(k).wait_send()
        rdma(dsend.at[lax.rem(d + k, ndp)], drecv.at[d], dn_send.at[k], dn_recv.at[d], (d, sib)).wait_send()
    own_to_sib.wait_send()
    for k in range(1, nchip):
        cg_copy(k).wait_send()
        cf_copy(k).wait_send()
    for a in range(2):
        for q in range(nchip):
            sib_copy(a, q).wait_send()
        for k in range(1, nchip):
            rs_copy(a, k).wait_send()

    @pl.loop(0, cb)
    def _(c):
        for n, g in enumerate((d, d, d, xp, xp, ym, yp_o)):
            h_copy(c, g, n, xp).wait_send()
            g_copy(c, g, n, xp).wait_send()


def on_device(tokens, grad_out, block_mask, gate_blocks, up_blocks, down_blocks):
    nt = lax.axis_size("tensor")
    ndp = lax.axis_size("dp")
    shard = lax.axis_index("tensor")
    rb = block_mask.shape[0]
    cb = block_mask.shape[1] // nt
    cap = gate_blocks.shape[0]
    m, width = tokens.shape
    nh = width // 2048
    group = m * nt
    ds = width // ndp
    nb = rb * cb
    cm = m * 2 * (ds // 128) // 16
    flags = lax.dynamic_slice_in_dim(block_mask, shard * cb, cb, 1).reshape(-1)
    pos = jnp.arange(nb, dtype=jnp.int32)
    upto = jnp.sum(jnp.where(pos[None, :] <= pos[:, None], flags[None, :], 0), axis=1)
    slot = jnp.where(flags > 0, upto - 1, cap)
    kept = jnp.sum((upto[None, :] <= jnp.arange(cap, dtype=jnp.int32)[:, None]).astype(jnp.int32), axis=1)

    vm = pl.BlockSpec(memory_space=pltpu.VMEM)
    sm = pl.BlockSpec(memory_space=pltpu.SMEM)
    hb = pl.BlockSpec(memory_space=pl.ANY)
    dma = pltpu.SemaphoreType.DMA
    own_rows = jax.ShapeDtypeStruct((m, width), BF)
    grad = jax.ShapeDtypeStruct((cap, 16, 128), BF)
    return pl.pallas_call(
        functools.partial(kernel, (ndp, nt, m, nh, rb, cb, cap)),
        out_shape=(own_rows, own_rows, grad, grad, grad),
        in_specs=[vm, vm, sm, sm, hb, hb, hb],
        out_specs=[vm] * 5,
        scratch_shapes=[
            pltpu.VMEM((cap + 1, 128, 128), BF),
            pltpu.VMEM((cap + 1, 128, 128), BF),
            pltpu.VMEM((cb, width, 256), BF),
            pltpu.VMEM((cb * 128, width), BF),
            pltpu.VMEM((2, 16, width), BF),
            pltpu.VMEM((2, group, nh, 16, 128), BF),
            pltpu.VMEM((2, group, width), BF),
            pltpu.VMEM((cb, group, 256), F32),
            pltpu.VMEM((cb, ndp, group, 128), BF),
            pltpu.VMEM((cb, ndp, group, 256), BF),
            pltpu.VMEM((group, cb * 128), BF),
            pltpu.VMEM((group, cb * 256), BF),
            pltpu.VMEM((2, nt // 2, m, nh, 16, 128), BF),
            pltpu.VMEM((2, nt // 2, m, nh, 16, 128), BF),
            pltpu.VMEM((16, nh, 16, 128), BF),
            pltpu.VMEM((ndp, cm, 16, 128), BF),
            pltpu.VMEM((ndp, cm, 16, 128), BF),
            pltpu.VMEM((ndp, nt * cm, 16, 128), BF),
            pltpu.VMEM((2, ndp, group, ds), BF),
            pltpu.VMEM((ds, ndp * group), BF),
            pltpu.VMEM((nb + 1, 16, 128), BF),
            pltpu.VMEM((nb + 1, 16, 128), BF),
            pltpu.VMEM((nb + 1, 16, 128), BF),
            pltpu.VMEM((ndp, cb, 16, ds), BF),
            pltpu.VMEM((ndp, cb, 16, ds), BF),
            pltpu.VMEM((256, 256), BF),
            dma((3,)),
            dma((2, nt // 2)),
            dma((2, nt)),
            dma((2, nt // 2)),
            dma((ndp,)),
            dma((ndp,)),
            dma((nt // 2,)),
            dma((nt,)),
            dma((nt // 2,)),
            dma((cb, 7)),
            dma((cb, ndp)),
            dma((cb, 7)),
            dma((cb, ndp)),
            dma((2, nt // 2)),
            dma((2, nt // 2)),
            dma((2, nt // 2)),
            dma((2, nt // 2)),
            dma((ndp,)),
            dma((ndp,)),
        ],
        compiler_params=pltpu.CompilerParams(
            collective_id=0, has_side_effects=True, vmem_limit_bytes=64 * 1024 * 1024
        ),
    )(tokens, grad_out, slot, kept, gate_blocks, up_blocks, down_blocks)


def solution(mesh):
    rows = P(("dp", "tensor"), None)
    blocks = P("tensor", None, None)
    grads = P("tensor", "dp", None)
    return jax.shard_map(
        on_device,
        mesh=mesh,
        in_specs=(rows, rows, P(), blocks, blocks, blocks),
        out_specs=(rows, rows, grads, grads, grads),
        check_vma=False,
    )
```

time: 140 us -> 113 us (0.81)
  Pallas kernels: 124 us -> 99.4 us
  local copies, waits for them, and re-layouts: 13.5 us -> 9.93 us
    pallas_call x1, Pallas kernels: 124 us -> 99.4 us  [on_device(): pl.pallas_call(functools.partial(kernel, (ndp, nt, m, nh, rb, cb, cap)),...]
    reshape x4 -> x0, local copies, waits for them, and re-layouts: 5.45 us -> none  [the longest x2 2.98 us: on_device(): gtok.reshape(m, ndp, rb, 16).transpose(0, 2, 1, 3).reshape(m, width)]
    unnamed x11 -> x5, local copies, waits for them, and re-layouts: 6.77 us -> 9.03 us
where the time goes in v2:
time: 113 us; the launch traced here: 111 us
  Pallas kernels  99.4 us (88%)
  local copies, waits for them, and re-layouts  9.93 us (9%)
  other arithmetic  1.37 us (1%)
    pallas_call x1, Pallas kernels, on_device(): pl.pallas_call(functools.partial(kernel, (ndp, nt, m, nh, rb, cb, cap)),...  99.4 us
    unnamed x5, local copies, waits for them, and re-layouts  9.03 us

profile of v2, /device:TPU:0, one launch (start us, length us, event | category | flops | bytes accessed | tf_op | source)
XLA Modules:
  0.0 111.3 jit_solution(13561887933023258997)
XLA Ops:
  0.6 0.8 constant_dynamic-slice_fusion
  1.4 0.1 reshape.15
  1.5 0.1 select_reduce_fusion
  1.7 0.6 compare_select_fusion.slot_ref
  2.2 0.7 convert_reduce_fusion.kept_ref
  2.9 99.4 %shard_map.101 = (bf16[10,4096]{1,0:T(8,128)(2,1)}, bf16[10,4096]{1,0:T(8,128)(2,1)}, bf16[140,16,128]{2,1,0:T(8,128)(2,1)}, bf16[140,16,128]{2,1,0:T(8,128)(2,1)}, bf16[140,16,128]{2,1,0:T(8,128)(2,1)}) custom-call(bf16[10,4096]{1,0:T(8,128)(2,1)} %tok_ref.1, bf16[10,4096]{1,0:T(8,128)(2,1)} %go_ref.1, s32[224]{0:T(256)} %compare_select_fusion.slot_ref, ...), custom_call_target="tpu_custom_call" | custom-call | tf_op jit(solution)/shard_map/pallas_call | solution.py:490
  102.3 1.6 %copy.16 = bf16[10,4096]{1,0:T(8,128)(2,1)} copy(bf16[10,4096]{1,0:T(8,128)(2,1)} %get-tuple-element.10) | data formatting | bytes 163840
  103.8 1.6 %copy.17 = bf16[10,4096]{1,0:T(8,128)(2,1)} copy(bf16[10,4096]{1,0:T(8,128)(2,1)} %get-tuple-element.11) | data formatting | bytes 163840
  105.4 2.0 %copy.18 = bf16[140,16,128]{2,1,0:T(8,128)(2,1)} copy(bf16[140,16,128]{2,1,0:T(8,128)(2,1)} %get-tuple-element.12) | data formatting | bytes 1146880
  107.4 2.0 %copy.19 = bf16[140,16,128]{2,1,0:T(8,128)(2,1)} copy(bf16[140,16,128]{2,1,0:T(8,128)(2,1)} %get-tuple-element.13) | data formatting | bytes 1146880
  109.3 2.0 %copy.20 = bf16[140,16,128]{2,1,0:T(8,128)(2,1)} copy(bf16[140,16,128]{2,1,0:T(8,128)(2,1)} %get-tuple-element.14) | data formatting | bytes 1146880

commit v3 on v2

--- a/solution.py
+++ b/solution.py
@@ -47,6 +47,7 @@
     ds = width // ndp
     nj = ds // 128
     nchip = nt // 2
+    nz = nchip // 2
     rpd = rb // ndp
     cm = m * 2 * nj // 16
     total = ndp * group
@@ -54,6 +55,7 @@
     s = lax.axis_index("tensor")
     y, x = d // 2, d % 2
     chip, core = s // 2, s % 2
+    z, xh = chip // 2, chip % 2
     ny = ndp // 2
 
     def rdma(src, dst, ssem, rsem, dev):
@@ -124,10 +126,12 @@
     def ag_arrived(a, src):
         rdma(chunk(a, src), chunk(a, src), ag_send.at[a, 0], ag_recv.at[a, src], (d, sib)).wait_recv()
 
-    for a in range(2):
+    def send_own(a):
         for k in range(1, nchip):
             ag_copy(a, k).start()
         fw_copy(a, 0).start()
+
+    send_own(0)
 
     def lay_inward(stage, lo):
         @pl.loop(0, rb)
@@ -139,6 +143,7 @@
     lay_inward(stage0, 0)
     load_d.start()
     load_u.wait()
+    send_own(1)
     lay_inward(stage1, 128)
 
     @pl.loop(0, ndp // 2)
@@ -187,6 +192,13 @@
                     lo = (h * 16 + j) * 128
                     rows[a, pl.ds(t0, 16), lo:lo + 128] = out[j * 16:(j + 1) * 16, h * 128:(h + 1) * 128]
 
+    load_d.wait()
+
+    @pl.loop(0, rb)
+    def _(r):
+        for c in range(cb):
+            wd[c * 128:(c + 1) * 128, pl.ds(pl.multiple_of(r * 128, 128), 128)] = stage0[slot_ref[r * cb + c]]
+
     forward(0)
     for k in range(nchip):
         ag_arrived(0, chip_behind(k) * 2 + (1 - core))
@@ -211,15 +223,41 @@
         hid[:, pl.ds(pl.multiple_of(c * 128, 128), 128)] = hidden
 
     forward(1)
-    load_d.wait()
-
-    @pl.loop(0, rb)
-    def _(r):
-        for c in range(cb):
-            wd[c * 128:(c + 1) * 128, pl.ds(pl.multiple_of(r * 128, 128), 128)] = stage0[slot_ref[r * cb + c]]
-
     for k in range(nchip):
         ag_arrived(1, chip_behind(k) * 2 + (1 - core))
+
+    for k in range(1, ndp):
+        src = lax.rem(d + k, ndp)
+        rdma(qrecv.at[src], qrecv.at[src], q_send.at[0], q_recv.at[src], (d, sib)).wait_recv()
+
+    def craw_of(src):
+        return craw.at[:, pl.ds(src * cm, cm)]
+
+    def at(kz, other, cr):
+        along = 1 - xh if other else xh
+        return (lax.rem(z + kz, nz) * 2 + along) * 2 + cr
+
+    def cg_copy(n, dst):
+        return rdma(qrecv, craw_of(s), cg_send.at[n], cg_recv.at[s], (d, dst))
+
+    def cz_copy(k):
+        src = at(0, True, core)
+        return rdma(craw_of(src), craw_of(src), cg_send.at[nz + k], cg_recv.at[src], (d, at(k, False, core)))
+
+    def cf_copy(k, other):
+        src = at(k, other, core)
+        return rdma(craw_of(src), craw_of(src), cf_send.at[k, other], cg_recv.at[src], (d, sib))
+
+    def cg_arrived(src):
+        rdma(craw_of(src), craw_of(src), cg_send.at[0], cg_recv.at[src], (d, sib)).wait_recv()
+
+    cg_copy(0, sib).start()
+    cg_copy(nz, at(0, True, core)).start()
+    for k in range(1, nz):
+        cg_copy(k, at(k, False, core)).start()
+    for g in range(ndp):
+        craw[g, pl.ds(s * cm, cm)] = qrecv[g]
+
     to_rows(1)
 
     @pl.loop(0, cb)
@@ -237,40 +275,6 @@
         g_copy(c, d, 2, ym).start()
         ggu[:, pl.ds(pl.multiple_of(c * 256, 128), 128)] = gga
         ggu[:, pl.ds(pl.multiple_of(c * 256 + 128, 128), 128)] = gua
-
-    @pl.loop(0, cb)
-    def _(c):
-        h_copy(c, xp, 0, xp).wait_recv()
-        h_copy(c, xp, 3, yp).start()
-        h_copy(c, xp, 4, ym).start()
-        h_copy(c, ym, 0, xp).wait_recv()
-        h_copy(c, ym, 5, yp).start()
-
-    for k in range(1, ndp):
-        src = lax.rem(d + k, ndp)
-        rdma(qrecv.at[src], qrecv.at[src], q_send.at[0], q_recv.at[src], (d, sib)).wait_recv()
-
-    def craw_of(src):
-        return craw.at[:, pl.ds(src * cm, cm)]
-
-    def cg_copy(k):
-        dst = chip_ahead(k) * 2 + core
-        return rdma(qrecv, craw_of(s), cg_send.at[k], cg_recv.at[s], (d, dst))
-
-    own_to_sib = rdma(qrecv, craw_of(s), cg_send.at[0], cg_recv.at[s], (d, sib))
-
-    def cf_copy(k):
-        src = chip_behind(k) * 2 + core
-        return rdma(craw_of(src), craw_of(src), cf_send.at[k], cg_recv.at[src], (d, sib))
-
-    def cg_arrived(src):
-        rdma(craw_of(src), craw_of(src), cg_send.at[0], cg_recv.at[src], (d, sib)).wait_recv()
-
-    for k in range(1, nchip):
-        cg_copy(k).start()
-    own_to_sib.start()
-    for g in range(ndp):
-        craw[g, pl.ds(s * cm, cm)] = qrecv[g]
 
     for a in range(2):
         for k in range(1, nchip):
@@ -303,6 +307,17 @@
     def sib_copy(a, q):
         return rdma(chunk(a, q * 2 + (1 - core)), sibx.at[a, q], sib_send.at[a, q], sib_recv.at[a, q], (d, sib))
 
+    @pl.loop(0, cb)
+    def _(c):
+        h_copy(c, xp, 0, xp).wait_recv()
+        h_copy(c, xp, 4, ym).start()
+        h_copy(c, xp, 3, yp).start()
+
+    cg_arrived(at(0, True, core))
+    for k in range(1, nz):
+        cz_copy(k).start()
+    cf_copy(0, 1).start()
+
     @pl.loop(0, width // step)
     def _(n):
         lo = pl.multiple_of(n * step, step)
@@ -314,23 +329,31 @@
     for q in range(nchip):
         sib_copy(0, q).start()
 
+    @pl.loop(0, cb)
+    def _(c):
+        h_copy(c, ym, 0, xp).wait_recv()
+        h_copy(c, ym, 5, yp).start()
+
     @pl.loop(0, width // step)
     def _(n):
         lo = pl.multiple_of(n * step, step)
         wide = jnp.concatenate([wgu[c, pl.ds(lo, step), :] for c in range(cb)], axis=1)
         rows[1, :, pl.ds(lo, step)] = nt_dot(ggu[...], wide).astype(BF)
 
+    @pl.loop(0, cb)
+    def _(c):
+        g_copy(c, xp, 0, xp).wait_recv()
+        g_copy(c, xp, 4, ym).start()
+        g_copy(c, xp, 3, yp).start()
+
     to_chunks(1)
     for q in range(nchip):
         sib_copy(1, q).start()
 
     @pl.loop(0, cb)
     def _(c):
-        g_copy(c, xp, 0, xp).wait_recv()
-        g_copy(c, xp, 3, yp).start()
-        g_copy(c, xp, 4, ym).start()
-        g_copy(c, ym, 0, xp).wait_recv()
-        g_copy(c, ym, 5, yp).start()
+        h_copy(c, yp_o, 0, xp).wait_recv()
+        h_copy(c, yp_o, 6, ym).start()
 
     def rs_copy(a, k):
         q = chip_ahead(k)
@@ -353,14 +376,16 @@
 
     @pl.loop(0, cb)
     def _(c):
-        h_copy(c, yp_o, 0, xp).wait_recv()
-        h_copy(c, yp_o, 6, ym).start()
-
-    for k in range(1, nchip):
-        cg_arrived(chip_behind(k) * 2 + core)
-        cf_copy(k).start()
-    for k in range(nchip):
-        cg_arrived(chip_behind(k) * 2 + (1 - core))
+        g_copy(c, ym, 0, xp).wait_recv()
+        g_copy(c, ym, 5, yp).start()
+
+    for k in range(1, nz):
+        for other in range(2):
+            cg_arrived(at(k, other, core))
+            cf_copy(k, other).start()
+    for k in range(nz):
+        for other in range(2):
+            cg_arrived(at(k, other, 1 - core))
 
     @pl.loop(0, ndp // 2)
     def _(gp):
@@ -382,11 +407,6 @@
     for q in range(total // 128):
         tokt[:, q * 128:(q + 1) * 128] = tall[q * 128:(q + 1) * 128].T
 
-    @pl.loop(0, cb)
-    def _(c):
-        g_copy(c, yp_o, 0, xp).wait_recv()
-        g_copy(c, yp_o, 6, ym).start()
-
     def dn_copy(c, k):
         dst = lax.rem(d + k, ndp)
         return rdma(dsend.at[dst, c], drecv.at[d, c], dn_send.at[k], dn_recv.at[d], (dst, s))
@@ -401,6 +421,11 @@
         for k in range(1, ndp):
             dn_copy(c, k).start()
         drecv[d, c] = dsend[d, c]
+
+    @pl.loop(0, cb)
+    def _(c):
+        g_copy(c, yp_o, 0, xp).wait_recv()
+        g_copy(c, yp_o, 6, ym).start()
 
     for a, out_ref in ((0, mixed_ref), (1, gtok_ref)):
         for k in range(1, nchip):
@@ -445,10 +470,14 @@
     for k in range(1, ndp):
         q_copy(k).wait_send()
         rdma(dsend.at[lax.rem(d + k, ndp)], drecv.at[d], dn_send.at[k], dn_recv.at[d], (d, sib)).wait_send()
-    own_to_sib.wait_send()
-    for k in range(1, nchip):
-        cg_copy(k).wait_send()
-        cf_copy(k).wait_send()
+    cg_copy(0, sib).wait_send()
+    cg_copy(nz, sib).wait_send()
+    cf_copy(0, 1).wait_send()
+    for k in range(1, nz):
+        cg_copy(k, sib).wait_send()
+        cz_copy(k).wait_send()
+        for other in range(2):
+            cf_copy(k, other).wait_send()
     for a in range(2):
         for q in range(nchip):
             sib_copy(a, q).wait_send()
@@ -460,6 +489,15 @@
         for n, g in enumerate((d, d, d, xp, xp, ym, yp_o)):
             h_copy(c, g, n, xp).wait_send()
             g_copy(c, g, n, xp).wait_send()
+
+
+def hand_out(n, *refs):
+    sems = refs[-1]
+    copies = [pltpu.make_async_copy(refs[i], refs[n + i], sems.at[i]) for i in range(n)]
+    for copy in copies:
+        copy.start()
+    for copy in copies:
+        copy.wait()
 
 
 def on_device(tokens, grad_out, block_mask, gate_blocks, up_blocks, down_blocks):
@@ -487,7 +525,7 @@
     dma = pltpu.SemaphoreType.DMA
     own_rows = jax.ShapeDtypeStruct((m, width), BF)
     grad = jax.ShapeDtypeStruct((cap, 16, 128), BF)
-    return pl.pallas_call(
+    results = pl.pallas_call(
         functools.partial(kernel, (ndp, nt, m, nh, rb, cb, cap)),
         out_shape=(own_rows, own_rows, grad, grad, grad),
         in_specs=[vm, vm, sm, sm, hb, hb, hb],
@@ -527,7 +565,7 @@
             dma((ndp,)),
             dma((nt // 2,)),
             dma((nt,)),
-            dma((nt // 2,)),
+            dma((nt // 4, 2)),
             dma((cb, 7)),
             dma((cb, ndp)),
             dma((cb, 7)),
@@ -543,6 +581,13 @@
             collective_id=0, has_side_effects=True, vmem_limit_bytes=64 * 1024 * 1024
         ),
     )(tokens, grad_out, slot, kept, gate_blocks, up_blocks, down_blocks)
+    return pl.pallas_call(
+        functools.partial(hand_out, 5),
+        out_shape=(own_rows, own_rows, grad, grad, grad),
+        in_specs=[hb] * 5,
+        out_specs=[hb] * 5,
+        scratch_shapes=[dma((5,))],
+    )(*results)
 
 
 def solution(mesh):

time: 113 us -> 163 us (1.44)
  Pallas kernels: 99.4 us -> 160 us
  local copies, waits for them, and re-layouts: 9.93 us -> 0.9 us
    pallas_call x0 -> x1, Pallas kernels: none -> 61.2 us  [on_device(): pl.pallas_call(functools.partial(hand_out, 5), out_shape=(own_rows, own_r...]
    unnamed x5 -> x0, local copies, waits for them, and re-layouts: 9.03 us -> none
where the time goes in v3:
time: 163 us
  Pallas kernels  160 us (98%)
    pallas_call x1, Pallas kernels, on_device(): pl.pallas_call(functools.partial(kernel, (ndp, nt, m, nh, rb, cb, cap)),...  98.4 us
    pallas_call x1, Pallas kernels, on_device(): pl.pallas_call(functools.partial(hand_out, 5), out_shape=(own_rows, own_r...  61.2 us

profile of v3, /device:TPU:0, one launch (start us, length us, event | category | flops | bytes accessed | tf_op | source)
XLA Modules:
  0.0 162.5 jit_solution(2997982601771457477)
XLA Ops:
  0.6 0.8 constant_dynamic-slice_fusion
  1.4 0.1 reshape.15
  1.5 0.1 select_reduce_fusion
  1.7 0.6 compare_select_fusion.slot_ref
  2.2 0.7 convert_reduce_fusion.kept_ref
  2.9 98.4 %shard_map.101 = (bf16[10,4096]{1,0:T(8,128)(2,1)}, bf16[10,4096]{1,0:T(8,128)(2,1)}, bf16[140,16,128]{2,1,0:T(8,128)(2,1)}, bf16[140,16,128]{2,1,0:T(8,128)(2,1)}, bf16[140,16,128]{2,1,0:T(8,128)(2,1)}) custom-call(bf16[10,4096]{1,0:T(8,128)(2,1)} %tok_ref.1, bf16[10,4096]{1,0:T(8,128)(2,1)} %go_ref.1, s32[224]{0:T(256)} %compare_select_fusion.slot_ref, ...), custom_call_target="tpu_custom_call" | custom-call | tf_op jit(solution)/shard_map/pallas_call | solution.py:528
  101.3 61.2 %shard_map.102 = (bf16[10,4096]{1,0:T(8,128)(2,1)}, bf16[10,4096]{1,0:T(8,128)(2,1)}, bf16[140,16,128]{2,1,0:T(8,128)(2,1)}, bf16[140,16,128]{2,1,0:T(8,128)(2,1)}, bf16[140,16,128]{2,1,0:T(8,128)(2,1)}) custom-call(bf16[10,4096]{1,0:T(8,128)(2,1)} %get-tuple-element.10.refs_0_, bf16[10,4096]{1,0:T(8,128)(2,1)} %get-tuple-element.11.refs_1_, ...), custom_call_target="tpu_custom_call" | custom-call | tf_op jit(solution)/shard_map/pallas_call | solution.py:584

commit v4 on v3

--- a/solution.py
+++ b/solution.py
@@ -51,6 +51,7 @@
     rpd = rb // ndp
     cm = m * 2 * nj // 16
     total = ndp * group
+    along_y = min(1, cb)
     d = lax.axis_index("dp")
     s = lax.axis_index("tensor")
     y, x = d // 2, d % 2
@@ -207,8 +208,16 @@
     def h_copy(c, g, n, dst):
         return rdma(acth.at[c, g], acth.at[c, g], h_send.at[c, n], h_recv.at[c, g], (dst, s))
 
+    def h_half(c, g, part, n, dst):
+        piece = acth.at[c, g, pl.ds(part * (group // 2), group // 2)]
+        return rdma(piece, piece, h_send.at[c, n], h_recv.at[c, g], (dst, s))
+
     def g_copy(c, g, n, dst):
         return rdma(actg.at[c, g], actg.at[c, g], g_send.at[c, n], g_recv.at[c, g], (dst, s))
+
+    def g_half(c, g, part, n, dst):
+        piece = actg.at[c, g, pl.ds(part * (group // 2), group // 2)]
+        return rdma(piece, piece, g_send.at[c, n], g_recv.at[c, g], (dst, s))
 
     @pl.loop(0, cb)
     def _(c):
@@ -307,7 +316,7 @@
     def sib_copy(a, q):
         return rdma(chunk(a, q * 2 + (1 - core)), sibx.at[a, q], sib_send.at[a, q], sib_recv.at[a, q], (d, sib))
 
-    @pl.loop(0, cb)
+    @pl.loop(along_y, cb)
     def _(c):
         h_copy(c, xp, 0, xp).wait_recv()
         h_copy(c, xp, 4, ym).start()
@@ -329,7 +338,16 @@
     for q in range(nchip):
         sib_copy(0, q).start()
 
-    @pl.loop(0, cb)
+    @pl.loop(0, along_y)
+    def _(c):
+        h_copy(c, ym, 0, xp).wait_recv()
+        h_half(c, ym, 0, 5, yp).start()
+        h_copy(c, ym, 3, xp).start()
+        h_copy(c, yp, 0, xp).wait_recv()
+        h_half(c, yp, 1, 6, ym).start()
+        h_copy(c, yp, 4, xp).start()
+
+    @pl.loop(along_y, cb)
     def _(c):
         h_copy(c, ym, 0, xp).wait_recv()
         h_copy(c, ym, 5, yp).start()
@@ -340,7 +358,7 @@
         wide = jnp.concatenate([wgu[c, pl.ds(lo, step), :] for c in range(cb)], axis=1)
         rows[1, :, pl.ds(lo, step)] = nt_dot(ggu[...], wide).astype(BF)
 
-    @pl.loop(0, cb)
+    @pl.loop(along_y, cb)
     def _(c):
         g_copy(c, xp, 0, xp).wait_recv()
         g_copy(c, xp, 4, ym).start()
@@ -350,7 +368,12 @@
     for q in range(nchip):
         sib_copy(1, q).start()
 
-    @pl.loop(0, cb)
+    @pl.loop(0, along_y)
+    def _(c):
+        h_copy(c, y2, 0, xp).wait_recv()
+        h_copy(c, y2, 7, xp).start()
+
+    @pl.loop(along_y, cb)
     def _(c):
         h_copy(c, yp_o, 0, xp).wait_recv()
         h_copy(c, yp_o, 6, ym).start()
@@ -374,7 +397,16 @@
                 chunks[a, mine] = both
                 rs_copy(a, k).start()
 
-    @pl.loop(0, cb)
+    @pl.loop(0, along_y)
+    def _(c):
+        g_copy(c, ym, 0, xp).wait_recv()
+        g_half(c, ym, 0, 5, yp).start()
+        g_copy(c, ym, 3, xp).start()
+        g_copy(c, yp, 0, xp).wait_recv()
+        g_half(c, yp, 1, 6, ym).start()
+        g_copy(c, yp, 4, xp).start()
+
+    @pl.loop(along_y, cb)
     def _(c):
         g_copy(c, ym, 0, xp).wait_recv()
         g_copy(c, ym, 5, yp).start()
@@ -411,10 +443,7 @@
         dst = lax.rem(d + k, ndp)
         return rdma(dsend.at[dst, c], drecv.at[d, c], dn_send.at[k], dn_recv.at[d], (dst, s))
 
-    @pl.loop(0, cb)
-    def _(c):
-        for g in (ym_o, yp, y2, y2_o):
-            h_copy(c, g, 0, xp).wait_recv()
+    def grad_down(c):
         down = tn_dot(acth[c].reshape(total, 128), cols[1].reshape(total, ds)).astype(BF)
         for o in range(ndp):
             dsend[o, c] = down[o * 16:(o + 1) * 16]
@@ -422,7 +451,24 @@
             dn_copy(c, k).start()
         drecv[d, c] = dsend[d, c]
 
-    @pl.loop(0, cb)
+    @pl.loop(0, along_y)
+    def _(c):
+        for g in (xp, ym_o, yp_o, y2_o):
+            h_copy(c, g, 0, xp).wait_recv()
+        grad_down(c)
+
+    @pl.loop(along_y, cb)
+    def _(c):
+        for g in (ym_o, yp, y2, y2_o):
+            h_copy(c, g, 0, xp).wait_recv()
+        grad_down(c)
+
+    @pl.loop(0, along_y)
+    def _(c):
+        g_copy(c, y2, 0, xp).wait_recv()
+        g_copy(c, y2, 7, xp).start()
+
+    @pl.loop(along_y, cb)
     def _(c):
         g_copy(c, yp_o, 0, xp).wait_recv()
         g_copy(c, yp_o, 6, ym).start()
@@ -439,14 +485,23 @@
                 lo = (h * 16 + j) * 128
                 out_ref[:, lo:lo + 128] = out[j * 16:j * 16 + m, h * 128:(h + 1) * 128]
 
-    @pl.loop(0, cb)
-    def _(c):
-        for g in (ym_o, yp, y2, y2_o):
-            g_copy(c, g, 0, xp).wait_recv()
+    def grad_inward(c):
         both = jnp.dot(tokt[...], actg[c].reshape(total, 256), preferred_element_type=F32).astype(BF)
         for r in range(rb):
             gblk[r * cb + c] = both[r * 16:(r + 1) * 16, :128]
             ublk[r * cb + c] = both[r * 16:(r + 1) * 16, 128:]
+
+    @pl.loop(0, along_y)
+    def _(c):
+        for g in (xp, ym_o, yp_o, y2_o):
+            g_copy(c, g, 0, xp).wait_recv()
+        grad_inward(c)
+
+    @pl.loop(along_y, cb)
+    def _(c):
+        for g in (ym_o, yp, y2, y2_o):
+            g_copy(c, g, 0, xp).wait_recv()
+        grad_inward(c)
 
     zero = jnp.zeros((16, 128), BF)
     gblk[rb * cb] = zero
@@ -484,7 +539,16 @@
         for k in range(1, nchip):
             rs_copy(a, k).wait_send()
 
-    @pl.loop(0, cb)
+    @pl.loop(0, along_y)
+    def _(c):
+        for n, g in ((0, d), (1, d), (2, d), (3, ym), (4, yp), (7, y2)):
+            h_copy(c, g, n, xp).wait_send()
+            g_copy(c, g, n, xp).wait_send()
+        for n, g in ((5, ym), (6, yp)):
+            h_half(c, g, 0, n, xp).wait_send()
+            g_half(c, g, 0, n, xp).wait_send()
+
+    @pl.loop(along_y, cb)
     def _(c):
         for n, g in enumerate((d, d, d, xp, xp, ym, yp_o)):
             h_copy(c, g, n, xp).wait_send()
@@ -492,12 +556,16 @@
 
 
 def hand_out(n, *refs):
-    sems = refs[-1]
-    copies = [pltpu.make_async_copy(refs[i], refs[n + i], sems.at[i]) for i in range(n)]
-    for copy in copies:
-        copy.start()
-    for copy in copies:
-        copy.wait()
+    given, results, held, sems = refs[:n], refs[n:2 * n], refs[2 * n:3 * n], refs[3 * n]
+    loads = [pltpu.make_async_copy(given[i], held[i], sems.at[0, i]) for i in range(n)]
+    stores = [pltpu.make_async_copy(held[i], results[i], sems.at[1, i]) for i in range(n)]
+    for load in loads:
+        load.start()
+    for load, store in zip(loads, stores):
+        load.wait()
+        store.start()
+    for store in stores:
+        store.wait()
 
 
 def on_device(tokens, grad_out, block_mask, gate_blocks, up_blocks, down_blocks):
@@ -566,9 +634,9 @@
             dma((nt // 2,)),
             dma((nt,)),
             dma((nt // 4, 2)),
-            dma((cb, 7)),
+            dma((cb, 8)),
             dma((cb, ndp)),
-            dma((cb, 7)),
+            dma((cb, 8)),
             dma((cb, ndp)),
             dma((2, nt // 2)),
             dma((2, nt // 2)),
@@ -586,7 +654,8 @@
         out_shape=(own_rows, own_rows, grad, grad, grad),
         in_specs=[hb] * 5,
         out_specs=[hb] * 5,
-        scratch_shapes=[dma((5,))],
+        scratch_shapes=[pltpu.VMEM(out.shape, BF) for out in (own_rows, own_rows, grad, grad, grad)]
+        + [dma((2, 5))],
     )(*results)
 
 

time: 163 us -> 100 us (0.61)
  Pallas kernels: 160 us -> 97.1 us
    pallas_call x1, Pallas kernels: 61.2 us -> 2.47 us  [on_device(): pl.pallas_call(functools.partial(hand_out, 5), out_shape=(own_rows, own_r...]
    pallas_call x1, Pallas kernels: 98.4 us -> 94.6 us  [on_device(): pl.pallas_call(functools.partial(kernel, (ndp, nt, m, nh, rb, cb, cap)),...]
where the time goes in v4:
time: 100 us
  Pallas kernels  97.1 us (97%)
  other arithmetic  1.37 us (1%)
    pallas_call x1, Pallas kernels, on_device(): pl.pallas_call(functools.partial(kernel, (ndp, nt, m, nh, rb, cb, cap)),...  94.6 us
    pallas_call x1, Pallas kernels, on_device(): pl.pallas_call(functools.partial(hand_out, 5), out_shape=(own_rows, own_r...  2.47 us

profile of v4, /device:TPU:0, one launch (start us, length us, event | category | flops | bytes accessed | tf_op | source)
XLA Modules:
  0.0 100.0 jit_solution(1315216509137911834)
XLA Ops:
  0.6 0.8 constant_dynamic-slice_fusion
  1.4 0.1 reshape.15
  1.5 0.1 select_reduce_fusion
  1.7 0.6 compare_select_fusion.slot_ref
  2.2 0.7 convert_reduce_fusion.kept_ref
  2.9 94.6 %shard_map.101 = (bf16[10,4096]{1,0:T(8,128)(2,1)}, bf16[10,4096]{1,0:T(8,128)(2,1)}, bf16[140,16,128]{2,1,0:T(8,128)(2,1)}, bf16[140,16,128]{2,1,0:T(8,128)(2,1)}, bf16[140,16,128]{2,1,0:T(8,128)(2,1)}) custom-call(bf16[10,4096]{1,0:T(8,128)(2,1)} %tok_ref.1, bf16[10,4096]{1,0:T(8,128)(2,1)} %go_ref.1, s32[224]{0:T(256)} %compare_select_fusion.slot_ref, ...), custom_call_target="tpu_custom_call" | custom-call | tf_op jit(solution)/shard_map/pallas_call | solution.py:596
  97.5 2.5 %shard_map.102 = (bf16[10,4096]{1,0:T(8,128)(2,1)}, bf16[10,4096]{1,0:T(8,128)(2,1)}, bf16[140,16,128]{2,1,0:T(8,128)(2,1)}, bf16[140,16,128]{2,1,0:T(8,128)(2,1)}, bf16[140,16,128]{2,1,0:T(8,128)(2,1)}) custom-call(bf16[10,4096]{1,0:T(8,128)(2,1)} %get-tuple-element.10.refs_0_, bf16[10,4096]{1,0:T(8,128)(2,1)} %get-tuple-element.11.refs_1_, ...), custom_call_target="tpu_custom_call" | custom-call | tf_op jit(solution)/shard_map/pallas_call | solution.py:652

commit v5 on v4

--- a/solution.py
+++ b/solution.py
@@ -51,7 +51,7 @@
     rpd = rb // ndp
     cm = m * 2 * nj // 16
     total = ndp * group
-    along_y = min(1, cb)
+    along_h, along_g = min(2, cb), min(1, cb)
     d = lax.axis_index("dp")
     s = lax.axis_index("tensor")
     y, x = d // 2, d % 2
@@ -316,7 +316,7 @@
     def sib_copy(a, q):
         return rdma(chunk(a, q * 2 + (1 - core)), sibx.at[a, q], sib_send.at[a, q], sib_recv.at[a, q], (d, sib))
 
-    @pl.loop(along_y, cb)
+    @pl.loop(along_h, cb)
     def _(c):
         h_copy(c, xp, 0, xp).wait_recv()
         h_copy(c, xp, 4, ym).start()
@@ -338,7 +338,7 @@
     for q in range(nchip):
         sib_copy(0, q).start()
 
-    @pl.loop(0, along_y)
+    @pl.loop(0, along_h)
     def _(c):
         h_copy(c, ym, 0, xp).wait_recv()
         h_half(c, ym, 0, 5, yp).start()
@@ -347,7 +347,7 @@
         h_half(c, yp, 1, 6, ym).start()
         h_copy(c, yp, 4, xp).start()
 
-    @pl.loop(along_y, cb)
+    @pl.loop(along_h, cb)
     def _(c):
         h_copy(c, ym, 0, xp).wait_recv()
         h_copy(c, ym, 5, yp).start()
@@ -358,7 +358,7 @@
         wide = jnp.concatenate([wgu[c, pl.ds(lo, step), :] for c in range(cb)], axis=1)
         rows[1, :, pl.ds(lo, step)] = nt_dot(ggu[...], wide).astype(BF)
 
-    @pl.loop(along_y, cb)
+    @pl.loop(along_g, cb)
     def _(c):
         g_copy(c, xp, 0, xp).wait_recv()
         g_copy(c, xp, 4, ym).start()
@@ -368,12 +368,12 @@
     for q in range(nchip):
         sib_copy(1, q).start()
 
-    @pl.loop(0, along_y)
+    @pl.loop(0, along_h)
     def _(c):
         h_copy(c, y2, 0, xp).wait_recv()
         h_copy(c, y2, 7, xp).start()
 
-    @pl.loop(along_y, cb)
+    @pl.loop(along_h, cb)
     def _(c):
         h_copy(c, yp_o, 0, xp).wait_recv()
         h_copy(c, yp_o, 6, ym).start()
@@ -397,7 +397,7 @@
                 chunks[a, mine] = both
                 rs_copy(a, k).start()
 
-    @pl.loop(0, along_y)
+    @pl.loop(0, along_g)
     def _(c):
         g_copy(c, ym, 0, xp).wait_recv()
         g_half(c, ym, 0, 5, yp).start()
@@ -406,7 +406,7 @@
         g_half(c, yp, 1, 6, ym).start()
         g_copy(c, yp, 4, xp).start()
 
-    @pl.loop(along_y, cb)
+    @pl.loop(along_g, cb)
     def _(c):
         g_copy(c, ym, 0, xp).wait_recv()
         g_copy(c, ym, 5, yp).start()
@@ -451,24 +451,24 @@
             dn_copy(c, k).start()
         drecv[d, c] = dsend[d, c]
 
-    @pl.loop(0, along_y)
+    @pl.loop(0, along_h)
     def _(c):
         for g in (xp, ym_o, yp_o, y2_o):
             h_copy(c, g, 0, xp).wait_recv()
         grad_down(c)
 
-    @pl.loop(along_y, cb)
+    @pl.loop(along_h, cb)
     def _(c):
         for g in (ym_o, yp, y2, y2_o):
             h_copy(c, g, 0, xp).wait_recv()
         grad_down(c)
 
-    @pl.loop(0, along_y)
+    @pl.loop(0, along_g)
     def _(c):
         g_copy(c, y2, 0, xp).wait_recv()
         g_copy(c, y2, 7, xp).start()
 
-    @pl.loop(along_y, cb)
+    @pl.loop(along_g, cb)
     def _(c):
         g_copy(c, yp_o, 0, xp).wait_recv()
         g_copy(c, yp_o, 6, ym).start()
@@ -491,13 +491,13 @@
             gblk[r * cb + c] = both[r * 16:(r + 1) * 16, :128]
             ublk[r * cb + c] = both[r * 16:(r + 1) * 16, 128:]
 
-    @pl.loop(0, along_y)
+    @pl.loop(0, along_g)
     def _(c):
         for g in (xp, ym_o, yp_o, y2_o):
             g_copy(c, g, 0, xp).wait_recv()
         grad_inward(c)
 
-    @pl.loop(along_y, cb)
+    @pl.loop(along_g, cb)
     def _(c):
         for g in (ym_o, yp, y2, y2_o):
             g_copy(c, g, 0, xp).wait_recv()
@@ -539,19 +539,28 @@
         for k in range(1, nchip):
             rs_copy(a, k).wait_send()
 
-    @pl.loop(0, along_y)
+    @pl.loop(0, along_h)
     def _(c):
         for n, g in ((0, d), (1, d), (2, d), (3, ym), (4, yp), (7, y2)):
             h_copy(c, g, n, xp).wait_send()
+        for n, g in ((5, ym), (6, yp)):
+            h_half(c, g, 0, n, xp).wait_send()
+
+    @pl.loop(along_h, cb)
+    def _(c):
+        for n, g in enumerate((d, d, d, xp, xp, ym, yp_o)):
+            h_copy(c, g, n, xp).wait_send()
+
+    @pl.loop(0, along_g)
+    def _(c):
+        for n, g in ((0, d), (1, d), (2, d), (3, ym), (4, yp), (7, y2)):
             g_copy(c, g, n, xp).wait_send()
         for n, g in ((5, ym), (6, yp)):
-            h_half(c, g, 0, n, xp).wait_send()
             g_half(c, g, 0, n, xp).wait_send()
 
-    @pl.loop(along_y, cb)
+    @pl.loop(along_g, cb)
     def _(c):
         for n, g in enumerate((d, d, d, xp, xp, ym, yp_o)):
-            h_copy(c, g, n, xp).wait_send()
             g_copy(c, g, n, xp).wait_send()
 
 

time: 100 us -> 98.9 us (0.989)
  Pallas kernels: 97.1 us -> 95.8 us
    pallas_call x1, Pallas kernels: 94.6 us -> 93.3 us  [on_device(): pl.pallas_call(functools.partial(kernel, (ndp, nt, m, nh, rb, cb, cap)),...]
where the time goes in v5:
time: 98.9 us; the launch traced here: 98.7 us
  Pallas kernels  95.8 us (97%)
  other arithmetic  1.37 us (1%)
    pallas_call x1, Pallas kernels, on_device(): pl.pallas_call(functools.partial(kernel, (ndp, nt, m, nh, rb, cb, cap)),...  93.3 us
    pallas_call x1, Pallas kernels, on_device(): pl.pallas_call(functools.partial(hand_out, 5), out_shape=(own_rows, own_r...  2.47 us

profile of v5, /device:TPU:0, one launch (start us, length us, event | category | flops | bytes accessed | tf_op | source)
XLA Modules:
  0.0 98.7 jit_solution(8973783179840136238)
XLA Ops:
  0.6 0.8 constant_dynamic-slice_fusion
  1.4 0.1 reshape.15
  1.5 0.1 select_reduce_fusion
  1.7 0.6 compare_select_fusion.slot_ref
  2.2 0.7 convert_reduce_fusion.kept_ref
  2.9 93.3 %shard_map.101 = (bf16[10,4096]{1,0:T(8,128)(2,1)}, bf16[10,4096]{1,0:T(8,128)(2,1)}, bf16[140,16,128]{2,1,0:T(8,128)(2,1)}, bf16[140,16,128]{2,1,0:T(8,128)(2,1)}, bf16[140,16,128]{2,1,0:T(8,128)(2,1)}) custom-call(bf16[10,4096]{1,0:T(8,128)(2,1)} %tok_ref.1, bf16[10,4096]{1,0:T(8,128)(2,1)} %go_ref.1, s32[224]{0:T(256)} %compare_select_fusion.slot_ref, ...), custom_call_target="tpu_custom_call" | custom-call | tf_op jit(solution)/shard_map/pallas_call | solution.py:605
  96.2 2.5 %shard_map.102 = (bf16[10,4096]{1,0:T(8,128)(2,1)}, bf16[10,4096]{1,0:T(8,128)(2,1)}, bf16[140,16,128]{2,1,0:T(8,128)(2,1)}, bf16[140,16,128]{2,1,0:T(8,128)(2,1)}, bf16[140,16,128]{2,1,0:T(8,128)(2,1)}) custom-call(bf16[10,4096]{1,0:T(8,128)(2,1)} %get-tuple-element.10.refs_0_, bf16[10,4096]{1,0:T(8,128)(2,1)} %get-tuple-element.11.refs_1_, ...), custom_call_target="tpu_custom_call" | custom-call | tf_op jit(solution)/shard_map/pallas_call | solution.py:661

commit v6 on v5

--- a/solution.py
+++ b/solution.py
@@ -439,6 +439,16 @@
     for q in range(total // 128):
         tokt[:, q * 128:(q + 1) * 128] = tall[q * 128:(q + 1) * 128].T
 
+    @pl.loop(0, along_g)
+    def _(c):
+        g_copy(c, y2, 0, xp).wait_recv()
+        g_copy(c, y2, 7, xp).start()
+
+    @pl.loop(along_g, cb)
+    def _(c):
+        g_copy(c, yp_o, 0, xp).wait_recv()
+        g_copy(c, yp_o, 6, ym).start()
+
     def dn_copy(c, k):
         dst = lax.rem(d + k, ndp)
         return rdma(dsend.at[dst, c], drecv.at[d, c], dn_send.at[k], dn_recv.at[d], (dst, s))
@@ -462,16 +472,6 @@
         for g in (ym_o, yp, y2, y2_o):
             h_copy(c, g, 0, xp).wait_recv()
         grad_down(c)
-
-    @pl.loop(0, along_g)
-    def _(c):
-        g_copy(c, y2, 0, xp).wait_recv()
-        g_copy(c, y2, 7, xp).start()
-
-    @pl.loop(along_g, cb)
-    def _(c):
-        g_copy(c, yp_o, 0, xp).wait_recv()
-        g_copy(c, yp_o, 6, ym).start()
 
     for a, out_ref in ((0, mixed_ref), (1, gtok_ref)):
         for k in range(1, nchip):

time: 98.9 us -> 98.9 us (level)
  no operation moved by 1% of the time
where the time goes in v6:
time: 98.9 us; the launch traced here: 98.7 us
  Pallas kernels  95.8 us (97%)
  other arithmetic  1.37 us (1%)
    pallas_call x1, Pallas kernels, on_device(): pl.pallas_call(functools.partial(kernel, (ndp, nt, m, nh, rb, cb, cap)),...  93.3 us
    pallas_call x1, Pallas kernels, on_device(): pl.pallas_call(functools.partial(hand_out, 5), out_shape=(own_rows, own_r...  2.47 us

profile of v6, /device:TPU:0, one launch (start us, length us, event | category | flops | bytes accessed | tf_op | source)
XLA Modules:
  0.0 98.7 jit_solution(4611344142817337557)
XLA Ops:
  0.6 0.8 constant_dynamic-slice_fusion
  1.4 0.1 reshape.15
  1.5 0.1 select_reduce_fusion
  1.7 0.6 compare_select_fusion.slot_ref
  2.2 0.7 convert_reduce_fusion.kept_ref
  2.9 93.3 %shard_map.101 = (bf16[10,4096]{1,0:T(8,128)(2,1)}, bf16[10,4096]{1,0:T(8,128)(2,1)}, bf16[140,16,128]{2,1,0:T(8,128)(2,1)}, bf16[140,16,128]{2,1,0:T(8,128)(2,1)}, bf16[140,16,128]{2,1,0:T(8,128)(2,1)}) custom-call(bf16[10,4096]{1,0:T(8,128)(2,1)} %tok_ref.1, bf16[10,4096]{1,0:T(8,128)(2,1)} %go_ref.1, s32[224]{0:T(256)} %compare_select_fusion.slot_ref, ...), custom_call_target="tpu_custom_call" | custom-call | tf_op jit(solution)/shard_map/pallas_call | solution.py:605
  96.2 2.5 %shard_map.102 = (bf16[10,4096]{1,0:T(8,128)(2,1)}, bf16[10,4096]{1,0:T(8,128)(2,1)}, bf16[140,16,128]{2,1,0:T(8,128)(2,1)}, bf16[140,16,128]{2,1,0:T(8,128)(2,1)}, bf16[140,16,128]{2,1,0:T(8,128)(2,1)}) custom-call(bf16[10,4096]{1,0:T(8,128)(2,1)} %get-tuple-element.10.refs_0_, bf16[10,4096]{1,0:T(8,128)(2,1)} %get-tuple-element.11.refs_1_, ...), custom_call_target="tpu_custom_call" | custom-call | tf_op jit(solution)/shard_map/pallas_call | solution.py:661
